TPU v7x, 128 devices: a whole 4x4x4 slice. The times are simulated.
128 devices in a mesh: section: 2 (over core), gx: 16 (over x, z), gy: 4 (over y).
Axes of the slice: x: 4, y: 4, z: 4, core: 2. Of those that a mesh axis runs over, the one named last changes fastest.
Arguments:
- inputs: bfloat16 [2, 2048, 768], P(None, ('gx', 'gy')), may hold values from -6 to 6
- cotangent: bfloat16 [2, 2048, 768], P(None, ('gx', 'gy')), may hold values from -6 to 6
- ln1_gain: float32 [2, 768], P('section'), may hold values from 0.25 to 1.75
- ln1_bias: float32 [2, 768], P('section'), may hold values from -3 to 3
- w_qkv: bfloat16 [2, 768, 3, 768], P('section', 'gx', None, 'gy'), may hold values from -0.21875 to 0.21875
- b_qv: float32 [2, 2, 768], P('section', None, 'gy'), may hold values from -3 to 3
- w_out: bfloat16 [2, 768, 768], P('section', 'gy', 'gx'), may hold values from -0.875 to 0.875
- b_out: float32 [2, 768], P('section'), may hold values from -3 to 3
- ln2_gain: float32 [2, 768], P('section'), may hold values from 0.25 to 1.75
- ln2_bias: float32 [2, 768], P('section'), may hold values from -3 to 3
- w_up: bfloat16 [2, 768, 3072], P('section', 'gx', 'gy'), may hold values from -0.21875 to 0.21875
- b_up: float32 [2, 3072], P('section', 'gy'), may hold values from -3 to 3
- w_down: bfloat16 [2, 3072, 768], P('section', 'gy', 'gx'), may hold values from -0.109375 to 0.109375
- b_down: float32 [2, 768], P('section'), may hold values from -3 to 3
Outputs:
- activations: bfloat16 [2, 2, 2048, 768], P('section', None, ('gx', 'gy'))
- input_grads: bfloat16 [2, 2, 2048, 768], P('section', None, ('gx', 'gy'))
- grad_ln1_gain: float32 [2, 768], P('section')
- grad_ln1_bias: float32 [2, 768], P('section')
- grad_w_qkv: float32 [2, 768, 3, 768], P('section', 'gx', None, 'gy')
- grad_b_qv: float32 [2, 2, 768], P('section', None, 'gy')
- grad_w_out: float32 [2, 768, 768], P('section', 'gy', 'gx')
- grad_b_out: float32 [2, 768], P('section')
- grad_ln2_gain: float32 [2, 768], P('section')
- grad_ln2_bias: float32 [2, 768], P('section')
- grad_w_up: float32 [2, 768, 3072], P('section', 'gx', 'gy')
- grad_b_up: float32 [2, 3072], P('section', 'gy')
- grad_w_down: float32 [2, 3072, 768], P('section', 'gy', 'gx')
- grad_b_down: float32 [2, 768], P('section')
All inputs are finite; a program needn't handle non-finite values.
Results may differ from a plain program's by a relative error of at most 0.02.
Values may be sent and summed in bfloat16 or wider, within the bound.
A program may use at most 128 MiB of HBM per device.

v0:
```python
import jax
import jax.numpy as jnp
from jax import lax
from jax.sharding import PartitionSpec as P

HD = 64


EPSILON = 1e-05
MASKED = -1e30


def shifted(value, axis, steps):
    count = lax.axis_size(axis)
    leading, last = (max(0, -steps), min(count, count - steps))
    return lax.ppermute(value, axis, [(source, source + steps) for source in range(leading, last)])


def norm_parts(values, gain, offset):
    average = jnp.mean(values, axis=-1, keepdims=True)
    centered = values - average
    variance = jnp.mean(centered * centered, axis=-1, keepdims=True)
    factor = lax.rsqrt(variance + EPSILON)
    unit_rows = centered * factor
    return (unit_rows * gain + offset, unit_rows, factor)


def norm_back(grad_rows, unit_rows, factor, gain):
    scaled = grad_rows * gain
    first_mean = jnp.mean(scaled, axis=-1, keepdims=True)
    second_mean = jnp.mean(scaled * unit_rows, axis=-1, keepdims=True)
    return factor * (scaled - first_mean - unit_rows * second_mean)


def gelu_tanh(values):
    return jax.nn.gelu(values, approximate=True)


def split_heads(columns):
    return columns.reshape(columns.shape[0], columns.shape[1] // HD, HD)


def block_scores(queries, key_block, query_start, key_start):
    raw_scores = (
        jnp.einsum("qhd,khd->hqk", queries, key_block, preferred_element_type=jnp.float32) * 0.125
    )
    query_pos = query_start + jnp.arange(queries.shape[0], dtype=jnp.int32)
    key_pos = key_start + jnp.arange(key_block.shape[0], dtype=jnp.int32)
    allowed = key_pos[None, :] <= query_pos[:, None]
    return jnp.where(allowed[None], raw_scores, MASKED)


def value_product(weights, scaled_grad):
    rounded = weights.astype(jnp.bfloat16)
    upper = scaled_grad.astype(jnp.bfloat16)
    rest = (scaled_grad - upper.astype(jnp.float32)).astype(jnp.bfloat16)
    first = jnp.einsum("hqk,qhd->khd", rounded, upper, preferred_element_type=jnp.float32)
    return first + jnp.einsum("hqk,qhd->khd", rounded, rest, preferred_element_type=jnp.float32)


def attend(queries, all_keys, all_values, query_start, block_count):
    tok_rows = queries.shape[0]
    head_count = queries.shape[1]

    def find_top(block_index, running):
        key_block = lax.dynamic_slice_in_dim(all_keys, block_index * tok_rows, tok_rows, 0)
        scores = block_scores(queries, key_block, query_start, block_index * tok_rows)
        return jnp.maximum(running, jnp.max(scores, axis=-1))

    largest = lax.fori_loop(
        0, block_count, find_top, jnp.full((head_count, tok_rows), MASKED, jnp.float32)
    )

    def add_block(block_index, carry):
        totals, summed = carry
        key_block = lax.dynamic_slice_in_dim(all_keys, block_index * tok_rows, tok_rows, 0)
        value_block = lax.dynamic_slice_in_dim(all_values, block_index * tok_rows, tok_rows, 0)
        scores = block_scores(queries, key_block, query_start, block_index * tok_rows)
        weights = jnp.exp(scores - largest[:, :, None])
        summed = summed + jnp.einsum(
            "hqk,khd->qhd",
            weights.astype(jnp.bfloat16),
            value_block,
            preferred_element_type=jnp.float32,
        )
        return (totals + jnp.sum(weights, axis=-1), summed)

    start_carry = (
        jnp.zeros((head_count, tok_rows), jnp.float32),
        jnp.zeros((tok_rows, head_count, HD), jnp.float32),
    )
    totals, summed = lax.fori_loop(0, block_count, add_block, start_carry)
    return (summed / jnp.transpose(totals)[:, :, None], largest, totals)


def attend_back(
    queries, all_keys, all_values, query_start, block_count, grad_mixed, attended, largest, totals
):
    tok_rows = queries.shape[0]
    head_count = queries.shape[1]
    local_width = head_count * HD
    delta = jnp.transpose(jnp.sum(grad_mixed.astype(jnp.float32) * attended, axis=-1))

    def score_grads(
        query_block,
        grad_block,
        key_block,
        value_block,
        first_query,
        key_start,
        top_block,
        total_block,
        delta_block,
    ):
        scores = block_scores(query_block, key_block, first_query, key_start)
        weights = jnp.exp(scores - top_block[:, :, None])
        products = jnp.einsum(
            "qhd,khd->hqk", grad_block, value_block, preferred_element_type=jnp.float32
        )
        grad_scores = (
            weights * (products - delta_block[:, :, None]) / total_block[:, :, None]
        ).astype(jnp.bfloat16)
        return (weights, grad_scores)

    def query_part(block_index, running):
        key_block = lax.dynamic_slice_in_dim(all_keys, block_index * tok_rows, tok_rows, 0)
        value_block = lax.dynamic_slice_in_dim(all_values, block_index * tok_rows, tok_rows, 0)
        _, grad_scores = score_grads(
            queries,
            grad_mixed,
            key_block,
            value_block,
            query_start,
            block_index * tok_rows,
            largest,
            totals,
            delta,
        )
        return running + jnp.einsum(
            "hqk,khd->qhd", grad_scores, key_block, preferred_element_type=jnp.float32
        )

    query_sum = lax.fori_loop(
        0, block_count, query_part, jnp.zeros((tok_rows, head_count, HD), jnp.float32)
    )
    grad_query = (query_sum * 0.125).reshape(tok_rows, local_width).astype(jnp.bfloat16)
    scaled_grad = grad_mixed.astype(jnp.float32) / jnp.transpose(totals)[:, :, None]
    key_block = all_keys
    value_block = all_values
    weights, grad_scores = score_grads(
        queries,
        grad_mixed,
        key_block,
        value_block,
        query_start,
        jnp.int32(0),
        largest,
        totals,
        delta,
    )
    grad_keys = (
        jnp.einsum("hqk,qhd->khd", grad_scores, queries, preferred_element_type=jnp.float32) * 0.125
    )
    grad_values = value_product(weights, scaled_grad)
    summed_terms = lax.psum_scatter(
        jnp.concatenate(
            [
                grad_keys.reshape(tok_rows * lax.axis_size("gx"), local_width),
                grad_values.reshape(tok_rows * lax.axis_size("gx"), local_width),
            ],
            axis=1,
        ).astype(jnp.bfloat16),
        "gx",
        scatter_dimension=0,
        tiled=True,
    ).astype(jnp.float32)
    grad_key = summed_terms[:, :local_width].astype(jnp.bfloat16)
    grad_value = summed_terms[:, local_width:].astype(jnp.bfloat16)
    return (grad_query, grad_key, grad_value)


def keep_slot(buffer, new_value, slot_id, is_valid):
    previous = lax.dynamic_index_in_dim(buffer, slot_id, 0, keepdims=False)
    return lax.dynamic_update_index_in_dim(
        buffer, jnp.where(is_valid, new_value, previous), slot_id, 0
    )


def take_slot(buffer, slot_id):
    return lax.dynamic_index_in_dim(buffer, slot_id, 0, keepdims=False)


def local(
    inputs,
    cotangent,
    ln1_gain,
    ln1_bias,
    w_qkv,
    b_qv,
    w_out,
    b_out,
    ln2_gain,
    ln2_bias,
    w_up,
    b_up,
    w_down,
    b_down,
):
    section_id = lax.axis_index("section")
    section_count = lax.axis_size("section")
    row_id = lax.axis_index("gx")
    column_id = lax.axis_index("gy")
    micro_count = inputs.shape[0]
    rows_part = inputs.shape[1]
    tok_rows = rows_part * lax.axis_size("gy")
    query_start = row_id * tok_rows
    block_count = row_id + 1
    gain_one = ln1_gain[0]
    offset_one = ln1_bias[0]
    gain_two = ln2_gain[0]
    offset_two = ln2_bias[0]
    bias_qv = b_qv[0]
    bias_out = b_out[0]
    bias_up = b_up[0]
    bias_down = b_down[0]
    full_qkv, full_out, full_up, full_down = (
        lax.all_gather(w_qkv[0], "gx", axis=0, tiled=True),
        lax.all_gather(w_out[0], "gx", axis=1, tiled=True),
        lax.all_gather(w_up[0], "gx", axis=0, tiled=True),
        lax.all_gather(w_down[0], "gx", axis=1, tiled=True),
    )
    model_width = full_qkv.shape[0]
    local_width = full_qkv.shape[2]
    hidden_width = full_up.shape[1]
    qkv_matrix = full_qkv.reshape(model_width, 3 * local_width)
    head_count = local_width // HD
    kept_inputs = jnp.zeros((micro_count, tok_rows, model_width), jnp.bfloat16)
    kept_queries = jnp.zeros((micro_count, tok_rows, local_width), jnp.bfloat16)
    kept_pairs = jnp.zeros((micro_count, tok_rows, 2 * local_width), jnp.bfloat16)
    kept_attended = jnp.zeros((micro_count, tok_rows, head_count, HD), jnp.float32)
    kept_largest = jnp.zeros((micro_count, head_count, tok_rows), jnp.float32)
    kept_totals = jnp.zeros((micro_count, head_count, tok_rows), jnp.float32)
    kept_middle = jnp.zeros((micro_count, tok_rows, model_width), jnp.float32)
    kept_upward = jnp.zeros((micro_count, tok_rows, hidden_width), jnp.float32)
    layer_outputs = jnp.zeros((micro_count, rows_part, model_width), jnp.bfloat16)
    received = jnp.zeros((rows_part, model_width), jnp.bfloat16)
    for tick_number in range(micro_count + section_count - 1):
        micro_index = tick_number - section_id
        is_valid = jnp.logical_and(micro_index >= 0, micro_index < micro_count)
        slot_id = jnp.clip(micro_index, 0, micro_count - 1)
        own_rows = take_slot(inputs, slot_id)
        current = jnp.where(section_id == 0, own_rows, received)
        full_input = lax.all_gather(current, "gy", axis=0, tiled=True)
        hidden_rows = full_input.astype(jnp.float32)
        normed, _, _ = norm_parts(hidden_rows, gain_one, offset_one)
        joined = jnp.dot(
            normed.astype(jnp.bfloat16), qkv_matrix, preferred_element_type=jnp.float32
        ).reshape(tok_rows, 3, local_width)
        queries = (joined[:, 0] + bias_qv[0]).astype(jnp.bfloat16)
        key_rows = joined[:, 1].astype(jnp.bfloat16)
        value_rows = (joined[:, 2] + bias_qv[1]).astype(jnp.bfloat16)
        pair_rows = jnp.concatenate([key_rows, value_rows], axis=1)
        sequence_pairs = lax.all_gather(pair_rows, "gx", axis=0, tiled=True)
        attended, largest, totals = attend(
            split_heads(queries),
            split_heads(sequence_pairs[:, :local_width]),
            split_heads(sequence_pairs[:, local_width:]),
            query_start,
            block_count,
        )
        mixed = attended.reshape(tok_rows, local_width).astype(jnp.bfloat16)
        projected = lax.psum(
            jnp.dot(mixed, full_out, preferred_element_type=jnp.float32).astype(jnp.bfloat16), "gy"
        ).astype(jnp.float32)
        middle = hidden_rows + projected + bias_out
        normed_two, _, _ = norm_parts(middle, gain_two, offset_two)
        upward = (
            jnp.dot(normed_two.astype(jnp.bfloat16), full_up, preferred_element_type=jnp.float32)
            + bias_up
        )
        active = gelu_tanh(upward).astype(jnp.bfloat16)
        branch = lax.psum_scatter(
            jnp.dot(active, full_down, preferred_element_type=jnp.float32).astype(jnp.bfloat16),
            "gy",
            scatter_dimension=0,
            tiled=True,
        ).astype(jnp.float32)
        result = (
            lax.dynamic_slice_in_dim(middle, column_id * rows_part, rows_part, 0)
            + branch
            + bias_down
        ).astype(jnp.bfloat16)
        kept_inputs = keep_slot(kept_inputs, full_input, slot_id, is_valid)
        kept_queries = keep_slot(kept_queries, queries, slot_id, is_valid)
        kept_pairs = keep_slot(kept_pairs, pair_rows, slot_id, is_valid)
        kept_attended = keep_slot(kept_attended, attended, slot_id, is_valid)
        kept_largest = keep_slot(kept_largest, largest, slot_id, is_valid)
        kept_totals = keep_slot(kept_totals, totals, slot_id, is_valid)
        kept_middle = keep_slot(kept_middle, middle, slot_id, is_valid)
        kept_upward = keep_slot(kept_upward, upward, slot_id, is_valid)
        layer_outputs = keep_slot(layer_outputs, result, slot_id, is_valid)
        received = shifted(result, "section", 1)
    grad_qkv = jnp.zeros((model_width, 3 * local_width), jnp.float32)
    grad_out = jnp.zeros((local_width, model_width), jnp.float32)
    grad_up = jnp.zeros((model_width, hidden_width), jnp.float32)
    grad_down = jnp.zeros((hidden_width, model_width), jnp.float32)
    gain_one_grad = jnp.zeros((model_width,), jnp.float32)
    offset_one_grad = jnp.zeros((model_width,), jnp.float32)
    bias_qv_grad = jnp.zeros((2, local_width), jnp.float32)
    bias_out_grad = jnp.zeros((model_width,), jnp.float32)
    gain_two_grad = jnp.zeros((model_width,), jnp.float32)
    offset_two_grad = jnp.zeros((model_width,), jnp.float32)
    bias_up_grad = jnp.zeros((hidden_width,), jnp.float32)
    bias_down_grad = jnp.zeros((model_width,), jnp.float32)
    input_grad_rows = jnp.zeros((micro_count, rows_part, model_width), jnp.bfloat16)
    arriving = jnp.zeros((rows_part, model_width), jnp.bfloat16)
    for tick_number in range(micro_count + section_count - 1):
        micro_index = tick_number - (section_count - 1 - section_id)
        is_valid = jnp.logical_and(micro_index >= 0, micro_index < micro_count)
        slot_id = jnp.clip(micro_index, 0, micro_count - 1)
        own_grads = take_slot(cotangent, slot_id)
        grad_result = jnp.where(section_id == section_count - 1, own_grads, arriving)
        full_input = take_slot(kept_inputs, slot_id)
        queries = take_slot(kept_queries, slot_id)
        sequence_pairs = lax.all_gather(take_slot(kept_pairs, slot_id), "gx", axis=0, tiled=True)
        attended = take_slot(kept_attended, slot_id)
        largest = take_slot(kept_largest, slot_id)
        totals = take_slot(kept_totals, slot_id)
        middle = take_slot(kept_middle, slot_id)
        upward = take_slot(kept_upward, slot_id)
        hidden_rows = full_input.astype(jnp.float32)
        normed, unit_one, factor_one = norm_parts(hidden_rows, gain_one, offset_one)
        normed_low = normed.astype(jnp.bfloat16)
        normed_two, unit_two, factor_two = norm_parts(middle, gain_two, offset_two)
        normed_two_low = normed_two.astype(jnp.bfloat16)
        active_rows, gelu_pull = jax.vjp(gelu_tanh, upward)
        active = active_rows.astype(jnp.bfloat16)
        grad_full = lax.all_gather(grad_result, "gy", axis=0, tiled=True)
        down_term = jnp.einsum("th,td->hd", active, grad_full, preferred_element_type=jnp.float32)
        grad_active = jnp.einsum(
            "td,hd->th", grad_full, full_down, preferred_element_type=jnp.float32
        )
        grad_upward = gelu_pull(grad_active)[0].astype(jnp.bfloat16)
        up_term = jnp.einsum(
            "td,th->dh", normed_two_low, grad_upward, preferred_element_type=jnp.float32
        )
        grad_normed_two = lax.psum(
            jnp.einsum(
                "th,dh->td", grad_upward, full_up, preferred_element_type=jnp.float32
            ).astype(jnp.bfloat16),
            "gy",
        ).astype(jnp.float32)
        grad_middle = grad_full.astype(jnp.float32) + norm_back(
            grad_normed_two, unit_two, factor_two, gain_two
        )
        grad_branch = grad_middle.astype(jnp.bfloat16)
        mixed = attended.reshape(tok_rows, local_width).astype(jnp.bfloat16)
        out_term = jnp.einsum("tc,td->cd", mixed, grad_branch, preferred_element_type=jnp.float32)
        grad_mixed = jnp.einsum(
            "td,cd->tc", grad_branch, full_out, preferred_element_type=jnp.float32
        ).astype(jnp.bfloat16)
        grad_query, grad_key, grad_value = attend_back(
            split_heads(queries),
            split_heads(sequence_pairs[:, :local_width]),
            split_heads(sequence_pairs[:, local_width:]),
            query_start,
            block_count,
            split_heads(grad_mixed),
            attended,
            largest,
            totals,
        )
        grad_joined = jnp.concatenate([grad_query, grad_key, grad_value], axis=1)
        qkv_term = jnp.einsum(
            "td,tc->dc", normed_low, grad_joined, preferred_element_type=jnp.float32
        )
        grad_normed = lax.psum(
            jnp.einsum(
                "tc,dc->td", grad_joined, qkv_matrix, preferred_element_type=jnp.float32
            ).astype(jnp.bfloat16),
            "gy",
        ).astype(jnp.float32)
        grad_input = grad_middle + norm_back(grad_normed, unit_one, factor_one, gain_one)
        grad_piece = lax.dynamic_slice_in_dim(
            grad_input, column_id * rows_part, rows_part, 0
        ).astype(jnp.bfloat16)
        grad_qkv = grad_qkv + jnp.where(is_valid, qkv_term, 0.0)
        grad_out = grad_out + jnp.where(is_valid, out_term, 0.0)
        grad_up = grad_up + jnp.where(is_valid, up_term, 0.0)
        grad_down = grad_down + jnp.where(is_valid, down_term, 0.0)
        gain_one_grad = gain_one_grad + jnp.where(
            is_valid, jnp.sum(grad_normed * unit_one, axis=0), 0.0
        )
        offset_one_grad = offset_one_grad + jnp.where(is_valid, jnp.sum(grad_normed, axis=0), 0.0)
        qv_sums = jnp.stack(
            [
                jnp.sum(grad_query.astype(jnp.float32), axis=0),
                jnp.sum(grad_value.astype(jnp.float32), axis=0),
            ]
        )
        bias_qv_grad = bias_qv_grad + jnp.where(is_valid, qv_sums, 0.0)
        bias_out_grad = bias_out_grad + jnp.where(is_valid, jnp.sum(grad_middle, axis=0), 0.0)
        gain_two_grad = gain_two_grad + jnp.where(
            is_valid, jnp.sum(grad_normed_two * unit_two, axis=0), 0.0
        )
        offset_two_grad = offset_two_grad + jnp.where(
            is_valid, jnp.sum(grad_normed_two, axis=0), 0.0
        )
        bias_up_grad = bias_up_grad + jnp.where(
            is_valid, jnp.sum(grad_upward.astype(jnp.float32), axis=0), 0.0
        )
        bias_down_grad = bias_down_grad + jnp.where(
            is_valid, jnp.sum(grad_full.astype(jnp.float32), axis=0), 0.0
        )
        input_grad_rows = keep_slot(input_grad_rows, grad_piece, slot_id, is_valid)
        arriving = shifted(grad_piece, "section", -1)
    summed_qkv, summed_out, summed_up, summed_down = (
        lax.psum_scatter(
            grad_qkv.astype(jnp.bfloat16), "gx", scatter_dimension=0, tiled=True
        ).astype(jnp.float32),
        lax.psum_scatter(
            grad_out.astype(jnp.bfloat16), "gx", scatter_dimension=1, tiled=True
        ).astype(jnp.float32),
        lax.psum_scatter(
            grad_up.astype(jnp.bfloat16), "gx", scatter_dimension=0, tiled=True
        ).astype(jnp.float32),
        lax.psum_scatter(
            grad_down.astype(jnp.bfloat16), "gx", scatter_dimension=1, tiled=True
        ).astype(jnp.float32),
    )
    small_sums = lax.psum(
        (
            gain_one_grad,
            offset_one_grad,
            bias_qv_grad,
            bias_out_grad,
            gain_two_grad,
            offset_two_grad,
            bias_up_grad,
            bias_down_grad,
        ),
        "gx",
    )
    row_part = summed_qkv.shape[0]
    return (
        layer_outputs[None],
        input_grad_rows[None],
        small_sums[0][None],
        small_sums[1][None],
        summed_qkv.reshape(1, row_part, 3, local_width),
        small_sums[2][None],
        summed_out[None],
        small_sums[3][None],
        small_sums[4][None],
        small_sums[5][None],
        summed_up[None],
        small_sums[6][None],
        summed_down[None],
        small_sums[7][None],
    )


def solution(mesh):
    placed = (
        P(None, ("gx", "gy"), None),
        P(None, ("gx", "gy"), None),
        P("section", None),
        P("section", None),
        P("section", "gx", None, "gy"),
        P("section", None, "gy"),
        P("section", "gy", "gx"),
        P("section", None),
        P("section", None),
        P("section", None),
        P("section", "gx", "gy"),
        P("section", "gy"),
        P("section", "gy", "gx"),
        P("section", None),
    )
    return jax.shard_map(
        local,
        mesh=mesh,
        in_specs=placed,
        out_specs=(
            P("section", None, ("gx", "gy"), None),
            P("section", None, ("gx", "gy"), None),
            P("section", None),
            P("section", None),
            P("section", "gx", None, "gy"),
            P("section", None, "gy"),
            P("section", "gy", "gx"),
            P("section", None),
            P("section", None),
            P("section", None),
            P("section", "gx", "gy"),
            P("section", "gy"),
            P("section", "gy", "gx"),
            P("section", None),
        ),
        check_vma=False,
    )
```

profile of v0, /device:TPU:0, one launch (start us, length us, event | category | flops | bytes accessed | tf_op | source)
XLA Modules:
  0.0 1685.5 jit_solution(12741970416875772502)
XLA Ops:
  7.3 26.6 %all-gather.1 = bf16[1,768,3,192]{3,1,2,0:T(8,128)(2,1)S(1)} all-gather(bf16[1,48,3,192]{3,1,2,0:T(8,128)(2,1)} %param.36), channel_id=3, replica_groups=mesh['section'=2,'gx'=16,'gy'=4] {'gx'}, dimensions={1}, use_global_device_ids=true | all-gather | bytes 940032 | tf_op jit(solution)/shard_map/all_gather | solution.py:227
  34.7 12.6 all-gather
  50.4 23.3 %all-gather.2 = bf16[1,192,768]{1,2,0:T(8,128)(2,1)S(1)} all-gather(bf16[1,192,48]{1,2,0:T(8,128)(2,1)S(1)} %copy-done.89), channel_id=4, replica_groups=mesh['section'=2,'gx'=16,'gy'=4] {'gx'}, dimensions={2}, use_global_device_ids=true | all-gather | bytes 313344 | tf_op jit(solution)/shard_map/all_gather | solution.py:228
  73.8 20.9 %all-gather.18.cloned.1.call-done = bf16[2048,384]{0,1:T(8,128)(2,1)} async-done(((bf16[128,384]{0,1:T(8,128)(2,1)}), bf16[2048,384]{0,1:T(8,128)(2,1)}) %all-gather.18.cloned.1.call-update) | async-done | bytes 1572880 | tf_op jit(solution)/shard_map/all_gather | solution.py:263
  102.9 76.2 %all-reduce.12.cloned.1.call-done = bf16[128,768]{1,0:T(8,128)(2,1)} async-done(((bf16[128,768]{1,0:T(8,128)(2,1)}), bf16[128,768]{1,0:T(8,128)(2,1)}) %all-reduce.12.cloned.1.call-update) | async-done | bytes 196624 | tf_op jit(solution)/shard_map/psum | solution.py:272
  181.0 44.2 %all-gather.24.cloned.1.call-done = bf16[1,768,768]{2,1,0:T(8,128)(2,1)} async-done(((bf16[1,48,768]{2,1,0:T(8,128)(2,1)}), bf16[1,768,768]{2,1,0:T(8,128)(2,1)}) %all-gather.24.cloned.1.call-update) | async-done | bytes 1179664 | tf_op jit(solution)/shard_map/all_gather | solution.py:229
  227.7 42.3 %all-gather.26.cloned.1.call-done = bf16[1,768,768]{1,2,0:T(8,128)(2,1)} async-done(((bf16[1,768,48]{1,2,0:T(8,128)(2,1)}), bf16[1,768,768]{1,2,0:T(8,128)(2,1)}) %all-gather.26.cloned.1.call-update) | async-done | bytes 1179664 | tf_op jit(solution)/shard_map/all_gather | solution.py:230
  274.0 18.6 %reduce-scatter.21.cloned.1.call-done = bf16[32,768]{1,0:T(8,128)(2,1)} async-done(((bf16[128,768]{1,0:T(8,128)(2,1)}), bf16[32,768]{1,0:T(8,128)(2,1)}) %reduce-scatter.21.cloned.1.call-update) | async-done | bytes 49168 | tf_op jit(solution)/shard_map/reduce_scatter | solution.py:282
  298.0 12.3 all_gather.54
  317.7 40.9 %all-gather.20.cloned.1.call-done = bf16[2048,384]{0,1:T(8,128)(2,1)} async-done(((bf16[128,384]{0,1:T(8,128)(2,1)}), bf16[2048,384]{0,1:T(8,128)(2,1)}) %all-gather.20.cloned.1.call-update) | async-done | bytes 1572880 | tf_op jit(solution)/shard_map/all_gather | solution.py:263
  368.0 89.0 %all-reduce.14.cloned.1.call-done = bf16[128,768]{1,0:T(8,128)(2,1)} async-done(((bf16[128,768]{1,0:T(8,128)(2,1)}), bf16[128,768]{1,0:T(8,128)(2,1)}) %all-reduce.14.cloned.1.call-update) | async-done | bytes 196624 | tf_op jit(solution)/shard_map/psum | solution.py:272
  471.2 15.9 reduce-scatter.23.cloned.1.call-done
  490.0 13.1 all-gather.5
  535.8 28.8 %all-gather.22.cloned.1.call-done = bf16[2048,384]{0,1:T(8,128)(2,1)} async-done(((bf16[128,384]{0,1:T(8,128)(2,1)}), bf16[2048,384]{0,1:T(8,128)(2,1)}) %all-gather.22.cloned.1.call-update) | async-done | bytes 1572880 | tf_op jit(solution)/shard_map/all_gather | solution.py:263
  575.1 36.9 %all-gather.28.cloned.1.call-done = bf16[1,2048,384]{1,2,0:T(8,128)(2,1)} async-done(((bf16[1,128,384]{1,2,0:T(8,128)(2,1)}), bf16[1,2048,384]{1,2,0:T(8,128)(2,1)}) %all-gather.28.cloned.1.call-update) | async-done | bytes 1572880 | tf_op jit(solution)/shard_map/all_gather | solution.py:325
  620.0 64.3 %all-reduce.16.cloned.1.call-done = bf16[128,768]{1,0:T(8,128)(2,1)} async-done(((bf16[128,768]{1,0:T(8,128)(2,1)}), bf16[128,768]{1,0:T(8,128)(2,1)}) %all-reduce.16.cloned.1.call-update) | async-done | bytes 196624 | tf_op jit(solution)/shard_map/psum | solution.py:272
  695.6 41.6 %all-reduce.18.cloned.1.call-done = bf16[128,768]{1,0:T(8,128)(2,1)} async-done(((bf16[128,768]{1,0:T(8,128)(2,1)}), bf16[128,768]{1,0:T(8,128)(2,1)}) %all-reduce.18.cloned.1.call-update) | async-done | bytes 196624 | tf_op jit(solution)/shard_map/psum | solution.py:347
  759.6 68.6 %reduce-scatter.31.cloned.1.call-done = bf16[128,384]{1,0:T(8,128)(2,1)} async-done(((bf16[2048,384]{1,0:T(8,128)(2,1)}), bf16[128,384]{1,0:T(8,128)(2,1)}) %reduce-scatter.31.cloned.1.call-update) | async-done | bytes 98320
  830.4 45.2 %all-gather.30.cloned.1.call-done = bf16[1,2048,384]{1,2,0:T(8,128)(2,1)} async-done(((bf16[1,128,384]{1,2,0:T(8,128)(2,1)}), bf16[1,2048,384]{1,2,0:T(8,128)(2,1)}) %all-gather.30.cloned.1.call-update) | async-done | bytes 1572880 | tf_op jit(solution)/shard_map/all_gather | solution.py:325
  878.2 40.2 %all-reduce.20.cloned.1.call-done = bf16[128,768]{1,0:T(8,128)(2,1)} async-done(((bf16[128,768]{1,0:T(8,128)(2,1)}), bf16[128,768]{1,0:T(8,128)(2,1)}) %all-reduce.20.cloned.1.call-update) | async-done | bytes 196624 | tf_op jit(solution)/shard_map/psum | solution.py:377
  925.7 12.2 all_gather.60
  942.5 39.9 %all-reduce.22.cloned.1.call-done = bf16[128,768]{1,0:T(8,128)(2,1)} async-done(((bf16[128,768]{1,0:T(8,128)(2,1)}), bf16[128,768]{1,0:T(8,128)(2,1)}) %all-reduce.22.cloned.1.call-update) | async-done | bytes 196624 | tf_op jit(solution)/shard_map/psum | solution.py:347
  1007.4 67.8 %reduce-scatter.33.cloned.1.call-done = bf16[128,384]{1,0:T(8,128)(2,1)} async-done(((bf16[2048,384]{1,0:T(8,128)(2,1)}), bf16[128,384]{1,0:T(8,128)(2,1)}) %reduce-scatter.33.cloned.1.call-update) | async-done | bytes 98320
  1080.5 38.4 %all-reduce.24.cloned.1.call-done = bf16[128,768]{1,0:T(8,128)(2,1)} async-done(((bf16[128,768]{1,0:T(8,128)(2,1)}), bf16[128,768]{1,0:T(8,128)(2,1)}) %all-reduce.24.cloned.1.call-update) | async-done | bytes 196624 | tf_op jit(solution)/shard_map/psum | solution.py:377
  1152.8 30.3 %all-reduce.26.cloned.1.call-done = bf16[128,768]{1,0:T(8,128)(2,1)} async-done(((bf16[128,768]{1,0:T(8,128)(2,1)}), bf16[128,768]{1,0:T(8,128)(2,1)}) %all-reduce.26.cloned.1.call-update) | async-done | bytes 196624 | tf_op jit(solution)/shard_map/psum | solution.py:347
  1194.3 37.2 %all-gather.32.cloned.1.call-done = bf16[1,2048,384]{1,2,0:T(8,128)(2,1)} async-done(((bf16[1,128,384]{1,2,0:T(8,128)(2,1)}), bf16[1,2048,384]{1,2,0:T(8,128)(2,1)}) %all-gather.32.cloned.1.call-update) | async-done | bytes 1572880 | tf_op jit(solution)/shard_map/all_gather | solution.py:325
  1267.8 61.6 %reduce-scatter.27.cloned.1.call-done = bf16[192,48]{0,1:T(8,128)(2,1)} async-done(((bf16[192,768]{0,1:T(8,128)(2,1)}), bf16[192,48]{0,1:T(8,128)(2,1)}) %reduce-scatter.27.cloned.1.call-update) | async-done | bytes 18448 | tf_op jit(solution)/shard_map/reduce_scatter | solution.py:421
  1330.8 74.4 %reduce-scatter.37.cloned.1.call-done = bf16[48,768]{1,0:T(8,128)(2,1)} async-done(((bf16[768,768]{1,0:T(8,128)(2,1)}), bf16[48,768]{1,0:T(8,128)(2,1)}) %reduce-scatter.37.cloned.1.call-update) | async-done | bytes 73744
  1407.1 74.2 %reduce-scatter.35.cloned.1.call-done = bf16[128,384]{1,0:T(8,128)(2,1)} async-done(((bf16[2048,384]{1,0:T(8,128)(2,1)}), bf16[128,384]{1,0:T(8,128)(2,1)}) %reduce-scatter.35.cloned.1.call-update) | async-done | bytes 98320
  1486.6 70.5 %reduce-scatter.29.cloned.1.call-done = bf16[48,768]{1,0:T(8,128)(2,1)} async-done(((bf16[768,768]{1,0:T(8,128)(2,1)}), bf16[48,768]{1,0:T(8,128)(2,1)}) %reduce-scatter.29.cloned.1.call-update) | async-done | bytes 73744 | tf_op jit(solution)/shard_map/reduce_scatter | solution.py:424
  1558.8 41.2 %all-reduce.28.cloned.1.call-done = bf16[128,768]{1,0:T(8,128)(2,1)} async-done(((bf16[128,768]{1,0:T(8,128)(2,1)}), bf16[128,768]{1,0:T(8,128)(2,1)}) %all-reduce.28.cloned.1.call-update) | async-done | bytes 196624 | tf_op jit(solution)/shard_map/psum | solution.py:377
  1601.4 74.5 %all-reduce.1 = (f32[1,768]{1,0:T(1,128)}, f32[1,768]{1,0:T(1,128)}, f32[1,2,192]{2,1,0:T(2,128)}, f32[1,768]{1,0:T(1,128)}, f32[1,768]{1,0:T(1,128)}, /*index=5...) all-reduce(f32[1,768]{1,0:T(1,128)S(1)} %broadcast_in_dim.424, ...), channel_id=1, replica_groups=mesh['section'=2,'gx'=16,'gy'=4] {'gx'}, use_global_device_ids=true, to_apply=%region_81.82 | all-reduce | flops 5760 | bytes 46080 | tf_op jit(solution)/shard_map/psum | solution.py:431
  (702 shorter events, 304.6 us)
Async XLA Ops:
  7.2 87.5 %all-gather.18.cloned.1.call-start = ((), (), s32[]{:S(2)}) async-start(), calls=%async_computation.10 | async-start | bytes 1671168 | tf_op jit(solution)/shard_map/all_gather | solution.py:263
  50.3 128.9 %all-reduce.12.cloned.1.call-start = ((), (), s32[]{:S(2)}) async-start(), calls=%async_computation.11 | async-start | bytes 393216 | tf_op jit(solution)/shard_map/psum | solution.py:272
  73.7 667.3 %copy-start.1 = (bf16[1,192,768]{1,2,0:T(8,128)(2,1)}, bf16[1,192,768]{1,2,0:T(8,128)(2,1)S(1)}, u32[]{:S(2)}) copy-start(bf16[1,192,768]{1,2,0:T(8,128)(2,1)S(1)} %all-gather.2) | copy-start | bytes 884740
  100.8 124.4 %all-gather.24.cloned.1.call-start = ((), (), s32[]{:S(2)}) async-start(), calls=%async_computation.27 | async-start | bytes 1253376 | tf_op jit(solution)/shard_map/all_gather | solution.py:229
  101.5 168.5 %all-gather.26.cloned.1.call-start = ((), (), s32[]{:S(2)}) async-start(), calls=%async_computation.28 | async-start | bytes 1253376 | tf_op jit(solution)/shard_map/all_gather | solution.py:230
  102.1 190.4 %reduce-scatter.21.cloned.1.call-start = ((), (), s32[]{:S(2)}) async-start(), calls=%async_computation.12 | async-start | bytes 245760 | tf_op jit(solution)/shard_map/reduce_scatter | solution.py:282
  272.6 85.9 %all-gather.20.cloned.1.call-start = ((), (), s32[]{:S(2)}) async-start(), calls=%async_computation.13 | async-start | bytes 1671168 | tf_op jit(solution)/shard_map/all_gather | solution.py:263
  294.7 2.5 collective-permute-start
  313.2 143.8 %all-reduce.14.cloned.1.call-start = ((), (), s32[]{:S(2)}) async-start(), calls=%async_computation.14 | async-start | bytes 393216 | tf_op jit(solution)/shard_map/psum | solution.py:272
  366.4 120.7 %reduce-scatter.23.cloned.1.call-start = ((), (), s32[]{:S(2)}) async-start(), calls=%async_computation.15 | async-start | bytes 245760 | tf_op jit(solution)/shard_map/reduce_scatter | solution.py:282
  466.0 98.6 %all-gather.22.cloned.1.call-start = ((), (), s32[]{:S(2)}) async-start(), calls=%async_computation.16 | async-start | bytes 1671168 | tf_op jit(solution)/shard_map/all_gather | solution.py:263
  488.7 14.4 collective-permute-start.1
  519.3 92.8 %all-gather.28.cloned.1.call-start = ((), (), s32[]{:S(2)}) async-start(), calls=%async_computation.29 | async-start | bytes 1671168 | tf_op jit(solution)/shard_map/all_gather | solution.py:325
  535.8 148.5 %all-reduce.16.cloned.1.call-start = ((), (), s32[]{:S(2)}) async-start(), calls=%async_computation.17 | async-start | bytes 393216 | tf_op jit(solution)/shard_map/psum | solution.py:272
  574.9 162.3 %all-reduce.18.cloned.1.call-start = ((), (), s32[]{:S(2)}) async-start(), calls=%async_computation.19 | async-start | bytes 393216 | tf_op jit(solution)/shard_map/psum | solution.py:347
  695.1 133.1 %reduce-scatter.31.cloned.1.call-start = ((), (), s32[]{:S(2)}) async-start(), calls=%async_computation.32 | async-start | bytes 1671168
  753.8 121.7 %all-gather.30.cloned.1.call-start = ((), (), s32[]{:S(2)}) async-start(), calls=%async_computation.30 | async-start | bytes 1671168 | tf_op jit(solution)/shard_map/all_gather | solution.py:325
  755.6 162.9 %all-reduce.20.cloned.1.call-start = ((), (), s32[]{:S(2)}) async-start(), calls=%async_computation.20 | async-start | bytes 393216 | tf_op jit(solution)/shard_map/psum | solution.py:377
  830.3 152.1 %all-reduce.22.cloned.1.call-start = ((), (), s32[]{:S(2)}) async-start(), calls=%async_computation.21 | async-start | bytes 393216 | tf_op jit(solution)/shard_map/psum | solution.py:347
  921.6 4.0 collective-permute-start.2
  941.0 134.2 %reduce-scatter.33.cloned.1.call-start = ((), (), s32[]{:S(2)}) async-start(), calls=%async_computation.33 | async-start | bytes 1671168
  1000.6 118.2 %all-reduce.24.cloned.1.call-start = ((), (), s32[]{:S(2)}) async-start(), calls=%async_computation.22 | async-start | bytes 393216 | tf_op jit(solution)/shard_map/psum | solution.py:377
  1078.1 105.0 %all-reduce.26.cloned.1.call-start = ((), (), s32[]{:S(2)}) async-start(), calls=%async_computation.23 | async-start | bytes 393216 | tf_op jit(solution)/shard_map/psum | solution.py:347
  1122.0 3.1 collective-permute-start.3
  1141.6 90.0 %all-gather.32.cloned.1.call-start = ((), (), s32[]{:S(2)}) async-start(), calls=%async_computation.31 | async-start | bytes 1671168 | tf_op jit(solution)/shard_map/all_gather | solution.py:325
  1142.2 111.6 %reduce-scatter.25.cloned.1.call-start = ((), (), s32[]{:S(2)}) async-start(), calls=%async_computation.18 | async-start | bytes 245760 | tf_op jit(solution)/shard_map/reduce_scatter | solution.py:282
  1149.4 180.0 %reduce-scatter.27.cloned.1.call-start = ((), (), s32[]{:S(2)}) async-start(), calls=%async_computation.25 | async-start | bytes 417792 | tf_op jit(solution)/shard_map/reduce_scatter | solution.py:421
  1188.1 217.1 %reduce-scatter.37.cloned.1.call-start = ((), (), s32[]{:S(2)}) async-start(), calls=%async_computation.35 | async-start | bytes 1253376
  1194.0 287.3 %reduce-scatter.35.cloned.1.call-start = ((), (), s32[]{:S(2)}) async-start(), calls=%async_computation.34 | async-start | bytes 1671168
  1246.8 310.4 %reduce-scatter.29.cloned.1.call-start = ((), (), s32[]{:S(2)}) async-start(), calls=%async_computation.26 | async-start | bytes 1253376 | tf_op jit(solution)/shard_map/reduce_scatter | solution.py:424
  1264.8 335.2 %all-reduce.28.cloned.1.call-start = ((), (), s32[]{:S(2)}) async-start(), calls=%async_computation.24 | async-start | bytes 393216 | tf_op jit(solution)/shard_map/psum | solution.py:377
  1483.4 193.2 %reduce-scatter.39.cloned.1.call-start = ((), (), s32[]{:S(2)}) async-start(), calls=%async_computation.36 | async-start | bytes 1044480
  (159 other events, 3027.8 us)
Sparse Core Ops, SparseCore 0:
  50.4 44.2 all-gather.17
  100.9 78.1 all-reduce.11
  181.5 43.6 all-gather.23
  227.5 42.4 all-gather.25
  272.7 19.7 reduce-scatter.20
  313.3 45.2 all-gather.19
  366.5 90.4 all-reduce.13
  466.2 20.9 reduce-scatter.22
  519.4 45.2 all-gather.21
  567.2 44.8 all-gather.27
  614.4 69.9 all-reduce.15
  695.3 41.8 all-reduce.17
  753.9 74.2 reduce-scatter.30
  830.8 44.6 all-gather.29
  877.7 40.7 all-reduce.19
  941.1 41.2 all-reduce.21
  1000.8 74.3 reduce-scatter.32
  1078.2 40.6 all-reduce.23
  1141.7 41.3 all-reduce.25
  1185.6 45.9 all-gather.31
  1233.9 19.7 reduce-scatter.24
  1257.2 72.1 reduce-scatter.26
  1332.6 72.5 reduce-scatter.36
  1408.3 72.9 reduce-scatter.34
  1484.5 72.5 reduce-scatter.28
  1559.3 40.6 all-reduce.27
  1603.4 73.1 reduce-scatter.38
where the time goes:
time: 1710 us; the launch traced here: 1690 us
  waiting for transfers between devices  1220 us (71%)
  blocking collectives  199 us (12%)
  matrix products  99 us (6%)
  other arithmetic  82.2 us (5%)
  local copies, waits for them, and re-layouts  62.7 us (4%)
    unnamed x32, waiting for transfers between devices  288 us
    psum x3, waiting for transfers between devices, local(): lax.psum(jnp.dot(mixed, full_out, preferred_element_type=jnp.float32).ast...  229 us
    psum x3, waiting for transfers between devices, local(): lax.psum(jnp.einsum('tc,dc->td', grad_joined, qkv_matrix, preferred_eleme...  120 us
    all_gather x3, waiting for transfers between devices, local(): lax.all_gather(take_slot(kept_pairs, slot_id), 'gx', axis=0, tiled=True)  119 us
    psum x3, waiting for transfers between devices, local(): lax.psum(jnp.einsum('th,dh->td', grad_upward, full_up, preferred_element_...  112 us
    all_gather x3, waiting for transfers between devices, local(): sequence_pairs = lax.all_gather(pair_rows, 'gx', axis=0, tiled=True)  90.6 us
    psum x1, blocking collectives, local(): lax.psum((gain_one_grad, offset_one_grad, bias_qv_grad, bias_out_grad, ga...  74.5 us
    reduce_scatter x1, waiting for transfers between devices, local(): lax.psum_scatter(grad_up.astype(jnp.bfloat16), 'gx', scatter_dimension=0,...  70.5 us
  transfers between devices with their start and end apart: 31, of which 29 were waited for; matrix products, arithmetic and copies ran while one was open for 8% of the time, Pallas kernels for 0%

commit v1 on v0

v1 whole, which is shorter than its diff:
```python
import jax
import jax.numpy as jnp
from jax import lax
from jax.experimental import pallas as pl
from jax.experimental.pallas import tpu as pltpu
from jax.sharding import PartitionSpec as P

HD = 64
EPSILON = 1e-05
MASKED = -1e30
MESH = pl.DeviceIdType.MESH
F32 = jnp.float32
BF16 = jnp.bfloat16

ROWS = 32
FULL = 128
D = 768
CHUNK = 512
HEADS = 3
STACK = HEADS * FULL

UP = slice(0, 768)
DOWN = slice(768, 1536)
KV = slice(1536, 1920)
QUERY = slice(1920, 2176)
OUT = slice(2048, 2304)
QUERY_OUT = slice(1920, 2304)
COLUMNS = 2304
HALF = COLUMNS // 2
SHARD = 48
SEMS = 200


def dot_nn(a, b):
    return lax.dot_general(a, b, (((1,), (0,)), ((), ())), preferred_element_type=F32)


def dot_nt(a, b):
    return lax.dot_general(a, b, (((1,), (1,)), ((), ())), preferred_element_type=F32)


def dot_tn(a, b):
    return lax.dot_general(a, b, (((0,), (0,)), ((), ())), preferred_element_type=F32)


def norm_parts(values, gain, offset):
    average = jnp.mean(values, axis=-1, keepdims=True)
    centered = values - average
    variance = jnp.mean(centered * centered, axis=-1, keepdims=True)
    factor = lax.rsqrt(variance + EPSILON)
    unit_rows = centered * factor
    return (unit_rows * gain + offset, unit_rows, factor)


def norm_back(grad_rows, unit_rows, factor, gain):
    scaled = grad_rows * gain
    first_mean = jnp.mean(scaled, axis=-1, keepdims=True)
    second_mean = jnp.mean(scaled * unit_rows, axis=-1, keepdims=True)
    return factor * (scaled - first_mean - unit_rows * second_mean)


def gelu_parts(values):
    scale = 0.7978845608028654
    inner = scale * (values + 0.044715 * values * values * values)
    bent = jnp.tanh(inner)
    active = 0.5 * values * (1.0 + bent)
    slope = 0.5 * (1.0 + bent) + 0.5 * values * (1.0 - bent * bent) * scale * (
        1.0 + 3.0 * 0.044715 * values * values
    )
    return active, slope


def column_sum(values):
    return jnp.sum(values, axis=0, keepdims=True)


def head_mask(head, first):
    lane = lax.broadcasted_iota(jnp.int32, (FULL, 256), 1)
    low = first + HD * head
    return jnp.logical_and(lane >= low, lane < low + HD)


def spread_heads(values, first):
    return jnp.concatenate(
        [jnp.where(head_mask(head, first), values, 0.0) for head in range(HEADS)], axis=0
    )


def join_heads(stacked, first):
    total = jnp.zeros((FULL, 256), F32)
    for head in range(HEADS):
        part = stacked[head * FULL : (head + 1) * FULL]
        total = total + jnp.where(head_mask(head, first), part, 0.0)
    return total


class Links:
    def __init__(self, send_sems, recv_sems):
        self.send_sems, self.recv_sems = send_sems, recv_sems
        self.count = 0
        self.sent = []
        self.section = lax.axis_index("section")
        self.row = lax.axis_index("gx")
        self.y = lax.axis_index("gy")
        self.x = self.row // 4
        self.z = self.row % 4

    def near(self, axis, steps):
        if axis == "s":
            return 1 - self.section
        return (getattr(self, axis) + (steps + 4)) % 4

    def device(self, axis, steps):
        s, x, z, y = self.section, self.x, self.z, self.y
        there = self.near(axis, steps)
        if axis == "s":
            s = there
        elif axis == "x":
            x = there
        elif axis == "z":
            z = there
        else:
            y = there
        return (s, x * 4 + z, y)

    def exchange(self, axis, steps, source, target, landing):
        index = self.count
        self.count += 1
        sems = (self.send_sems.at[index], self.recv_sems.at[index])
        copy = pltpu.make_async_remote_copy(
            source, target, *sems, device_id=self.device(axis, steps), device_id_type=MESH
        )
        copy.start()
        self.sent.append(copy)
        arrival = pltpu.make_async_remote_copy(
            landing, landing, *sems, device_id=self.device(axis, -steps), device_id_type=MESH
        )
        return arrival.wait_recv

    def barrier(self):
        barrier = pltpu.get_barrier_semaphore()
        peers = [("s", 1)] + [(axis, steps) for axis in "xyz" for steps in (1, 2, 3)]
        for axis, steps in peers:
            pl.semaphore_signal(
                barrier, inc=1, device_id=self.device(axis, steps), device_id_type=MESH
            )
        pl.semaphore_wait(barrier, len(peers))

    def finish(self):
        for copy in self.sent:
            copy.wait_send()
        self.sent = []


def wait_all(waits):
    for wait in waits:
        wait()


def gather_y(links, buffer):
    y = links.y
    return [
        links.exchange("y", steps, buffer.at[y], buffer.at[y], buffer.at[links.near("y", -steps)])
        for steps in (1, 3, 2)
    ]


def scatter_y(links, outgoing, incoming, partial):
    y = links.y
    outgoing[...] = partial.astype(BF16).reshape(4, ROWS, D)
    waits = [
        links.exchange(
            "y",
            steps,
            outgoing.at[links.near("y", steps)],
            incoming.at[y],
            incoming.at[links.near("y", -steps)],
        )
        for steps in (2, 1, 3)
    ]
    incoming[y] = outgoing[y]
    return waits


def sum_slots(buffer):
    total = buffer[0].astype(F32)
    for slot in range(1, 4):
        total = total + buffer[slot].astype(F32)
    return total


def kernel(
    inputs,
    cotangent,
    own_weights,
    own_params,
    activations,
    input_grads,
    weight_grads,
    param_grads,
    send_sems,
    recv_sems,
    weights,
    params,
    normed_one,
    normed_two,
    grad_outs,
    grad_branches,
    scatter_out,
    scatter_in,
    pairs,
    scores,
    probs,
    queries,
    totals,
    attended,
    hidden,
    middles,
    actives,
    slopes,
    pair_grads,
    pair_in_a,
    pair_in_b,
    pair_mid_a,
    pair_mid_b,
    pair_end_a,
    pair_end_b,
    grads,
    grads_cross,
    grads_in_a,
    grads_in_b,
    grads_mid_a,
    grads_mid_b,
    grads_end_a,
    grads_end_b,
    sums,
    sums_cross,
    sums_y,
    sums_z,
    sums_x,
    outputs,
    output_cross,
    in_grads,
    in_grad_cross,
):
    links = Links(send_sems, recv_sems)
    s, x, z, y, row = links.section, links.x, links.z, links.y, links.row
    other = 1 - s
    side_a, side_b = pl.ds(0, HALF), pl.ds(HALF, HALF)
    links.barrier()

    params[s] = own_params[...]
    params_wait = links.exchange("s", 1, params.at[s], params.at[s], params.at[other])

    weights[s, x, z] = own_weights[...]
    first_a = [
        links.exchange(
            "z",
            steps,
            weights.at[s, x, z, :, side_a],
            weights.at[s, x, z, :, side_a],
            weights.at[s, x, links.near("z", -steps), :, side_a],
        )
        for steps in (1, 3, 2)
    ]
    first_b = [
        links.exchange(
            "x",
            steps,
            weights.at[s, x, z, :, side_b],
            weights.at[s, x, z, :, side_b],
            weights.at[s, links.near("x", -steps), z, :, side_b],
        )
        for steps in (1, 3, 2)
    ]

    params_wait()

    def norm_rows(layer, current):
        hidden[layer] = current
        normed, _, _ = norm_parts(current, params[layer, 0:1, :], params[layer, 1:2, :])
        normed_one[layer, y] = normed.astype(BF16)
        return gather_y(links, normed_one.at[layer])

    normed_waits = norm_rows(0, inputs[s].astype(F32))

    wait_all(first_a)
    second_a = [
        links.exchange(
            "x",
            steps,
            weights.at[s, x, :, :, side_a],
            weights.at[s, x, :, :, side_a],
            weights.at[s, links.near("x", -steps), :, :, side_a],
        )
        for steps in (1, 3, 2)
    ]
    wait_all(first_b)
    second_b = [
        links.exchange(
            "z",
            steps,
            weights.at[s, :, z, :, side_b],
            weights.at[s, :, z, :, side_b],
            weights.at[s, :, links.near("z", -steps), :, side_b],
        )
        for steps in (1, 3, 2)
    ]
    crossings = [
        links.exchange(
            "s",
            1,
            weights.at[s, x, :, :, side_a],
            weights.at[s, x, :, :, side_a],
            weights.at[other, x, :, :, side_a],
        ),
        links.exchange(
            "s",
            1,
            weights.at[s, :, z, :, side_b],
            weights.at[s, :, z, :, side_b],
            weights.at[other, :, z, :, side_b],
        ),
    ]
    for index, steps in enumerate((1, 3, 2)):
        second_a[index]()
        came = links.near("x", -steps)
        crossings.append(
            links.exchange(
                "s",
                1,
                weights.at[s, came, :, :, side_a],
                weights.at[s, came, :, :, side_a],
                weights.at[other, came, :, :, side_a],
            )
        )
        second_b[index]()
        came = links.near("z", -steps)
        crossings.append(
            links.exchange(
                "s",
                1,
                weights.at[s, :, came, :, side_b],
                weights.at[s, :, came, :, side_b],
                weights.at[other, :, came, :, side_b],
            )
        )
    wait_all(crossings)

    def matrix(layer, columns):
        width = columns.stop - columns.start
        return weights[layer, :, :, :, columns].reshape(D, width)

    def forward(layer, normed_waits):
        wait_all(normed_waits)
        normed = normed_one[layer].reshape(FULL, D)
        pair = dot_nn(normed, matrix(layer, KV)) + params[layer, 7:8, 0:384]
        pairs[layer, x, z] = pair.astype(BF16)
        own = pairs.at[layer]
        low, high = pl.ds(0, 64), pl.ds(64, 64)
        pair_first_a = [
            links.exchange(
                "z",
                steps,
                own.at[x, z, low],
                own.at[x, z, low],
                own.at[x, links.near("z", -steps), low],
            )
            for steps in (1, 3, 2)
        ]
        pair_first_b = [
            links.exchange(
                "x",
                steps,
                own.at[x, z, high],
                own.at[x, z, high],
                own.at[links.near("x", -steps), z, high],
            )
            for steps in (1, 3, 2)
        ]
        query = dot_nn(normed, matrix(layer, QUERY)) + params[layer, 7:8, 384:640]
        query = query.astype(BF16).astype(F32) * 0.125
        queries[layer] = spread_heads(query, 0).astype(BF16)
        wait_all(pair_first_a)
        pair_second_a = [
            links.exchange(
                "x",
                steps,
                own.at[x, :, low],
                own.at[x, :, low],
                own.at[links.near("x", -steps), :, low],
            )
            for steps in (1, 3, 2)
        ]
        wait_all(pair_first_b)
        pair_second_b = [
            links.exchange(
                "z",
                steps,
                own.at[:, z, high],
                own.at[:, z, high],
                own.at[:, links.near("z", -steps), high],
            )
            for steps in (1, 3, 2)
        ]
        wait_all(pair_second_a)
        wait_all(pair_second_b)

        stacked = queries[layer]
        position = lax.broadcasted_iota(jnp.int32, (STACK, CHUNK), 0) % FULL + row * FULL
        column = lax.broadcasted_iota(jnp.int32, (STACK, CHUNK), 1)

        def find_top(chunk, running):
            keys = pairs[layer, chunk, :, :, 0:256].reshape(CHUNK, 256)
            raw = dot_nt(stacked, keys)
            raw = jnp.where(column + chunk * CHUNK <= position, raw, MASKED)
            scores[chunk] = raw
            return jnp.maximum(running, jnp.max(raw, axis=1, keepdims=True))

        top = lax.fori_loop(0, x + 1, find_top, jnp.full((STACK, 1), MASKED, F32))

        def add_chunk(chunk, carry):
            total, summed = carry
            weight = jnp.exp(scores[chunk] - top)
            rounded = weight.astype(BF16)
            probs[layer, chunk] = rounded
            values = pairs[layer, chunk, :, :, 128:384].reshape(CHUNK, 256)
            return (
                total + jnp.sum(weight, axis=1, keepdims=True),
                summed + dot_nn(rounded, values),
            )

        total, summed = lax.fori_loop(
            0, x + 1, add_chunk, (jnp.zeros((STACK, 1), F32), jnp.zeros((STACK, 256), F32))
        )
        totals[layer] = total
        attention = join_heads(summed / total, HD)
        attended[layer] = attention
        partial = dot_nt(attention.astype(BF16), matrix(layer, OUT))
        wait_all(scatter_y(links, scatter_out.at[layer, 0], scatter_in.at[layer, 0], partial))
        middle = hidden[layer] + sum_slots(scatter_in.at[layer, 0]) + params[layer, 2:3, :]
        middles[layer] = middle
        second, _, _ = norm_parts(middle, params[layer, 3:4, :], params[layer, 4:5, :])
        normed_two[layer, y] = second.astype(BF16)
        wait_all(gather_y(links, normed_two.at[layer]))
        upward = (
            dot_nn(normed_two[layer].reshape(FULL, D), matrix(layer, UP)) + params[layer, 6:7, :]
        )
        active, slope = gelu_parts(upward)
        actives[layer] = active.astype(BF16)
        slopes[layer] = slope
        partial = dot_nt(actives[layer], matrix(layer, DOWN))
        wait_all(scatter_y(links, scatter_out.at[layer, 1], scatter_in.at[layer, 1], partial))
        result = middle + sum_slots(scatter_in.at[layer, 1]) + params[layer, 5:6, :]
        outputs[layer] = result.astype(BF16)

    forward(0, normed_waits)
    forward(1, norm_rows(1, outputs[0].astype(F32)))
    output_wait = links.exchange("s", 1, outputs.at[other], output_cross, output_cross)

    def backward(layer, grad_rows):
        grad_outs[layer, y] = grad_rows
        waits = gather_y(links, grad_outs.at[layer])
        sums[layer, 5:6, :] = column_sum(grad_rows.astype(F32))
        gain_one, gain_two = params[layer, 0:1, :], params[layer, 3:4, :]
        _, unit_one, factor_one = norm_parts(hidden[layer], gain_one, gain_one)
        _, unit_two, factor_two = norm_parts(middles[layer], gain_two, gain_two)
        wait_all(waits)
        grad_full = grad_outs[layer].reshape(FULL, D)
        grad_up = (dot_nn(grad_full, matrix(layer, DOWN)) * slopes[layer]).astype(BF16)
        partial = dot_nt(grad_up, matrix(layer, UP))
        waits = scatter_y(links, scatter_out.at[layer, 2], scatter_in.at[layer, 2], partial)
        down_grad = dot_tn(grad_full, actives[layer])
        grads[layer, :, :, :, DOWN] = down_grad.astype(BF16).reshape(4, 4, SHARD, D)
        up_grad = dot_tn(normed_two[layer].reshape(FULL, D), grad_up)
        grads[layer, :, :, :, UP] = up_grad.astype(BF16).reshape(4, 4, SHARD, D)
        sums[layer, 6:7, :] = column_sum(grad_up.astype(F32))
        wait_all(waits)
        grad_two = sum_slots(scatter_in.at[layer, 2])
        grad_middle = grad_rows.astype(F32) + norm_back(grad_two, unit_two, factor_two, gain_two)
        grad_branches[layer, y] = grad_middle.astype(BF16)
        waits = gather_y(links, grad_branches.at[layer])
        sums[layer, 2:3, :] = column_sum(grad_middle)
        sums[layer, 3:4, :] = column_sum(grad_two * unit_two)
        sums[layer, 4:5, :] = column_sum(grad_two)
        wait_all(waits)
        branch_full = grad_branches[layer].reshape(FULL, D)
        grad_mixed = dot_nn(branch_full, matrix(layer, OUT)).astype(BF16).astype(F32)
        stacked_grad = spread_heads(grad_mixed, HD)
        delta = jnp.sum(spread_heads(grad_mixed * attended[layer], HD), axis=1, keepdims=True)
        inverse = 1.0 / totals[layer]
        scaled_grad = (stacked_grad * inverse).astype(BF16)
        stacked_grad = stacked_grad.astype(BF16)
        stacked = queries[layer]

        def chunk_back(chunk, summed):
            keys = pairs[layer, chunk, :, :, 0:256].reshape(CHUNK, 256)
            values = pairs[layer, chunk, :, :, 128:384].reshape(CHUNK, 256)
            weight = probs[layer, chunk]
            products = dot_nt(stacked_grad, values)
            score_grad = (weight.astype(F32) * (products - delta) * inverse).astype(BF16)
            key_grad = dot_tn(score_grad, stacked)
            value_grad = dot_tn(weight, scaled_grad)
            joined = jnp.concatenate(
                [
                    key_grad[:, :128],
                    key_grad[:, 128:] + value_grad[:, :128],
                    value_grad[:, 128:],
                ],
                axis=1,
            )
            pair_grads[layer, chunk] = joined.astype(BF16).reshape(4, FULL, 384)
            return summed + dot_nn(score_grad, keys)

        def chunk_clear(chunk, carry):
            pair_grads[layer, chunk] = jnp.zeros((4, FULL, 384), BF16)
            return carry

        lax.fori_loop(x + 1, 4, chunk_clear, 0)
        query_sum = lax.fori_loop(0, x + 1, chunk_back, jnp.zeros((STACK, 256), F32))
        own = pair_grads.at[layer]
        low, high = pl.ds(0, 64), pl.ds(64, 64)
        waits_a = [
            links.exchange(
                "x",
                steps,
                own.at[links.near("x", steps), :, low],
                pair_in_a.at[layer, x],
                pair_in_a.at[layer, links.near("x", -steps)],
            )
            for steps in (2, 1, 3)
        ]
        waits_b = [
            links.exchange(
                "z",
                steps,
                own.at[:, links.near("z", steps), high],
                pair_in_b.at[layer, z],
                pair_in_b.at[layer, links.near("z", -steps)],
            )
            for steps in (2, 1, 3)
        ]
        pair_in_a[layer, x] = pair_grads[layer, x, :, 0:64]
        pair_in_b[layer, z] = pair_grads[layer, :, z, 64:128]
        grad_query = (join_heads(query_sum, 0) * 0.125).astype(BF16)
        normed = normed_one[layer].reshape(FULL, D)
        query_grad = dot_tn(normed, grad_query)
        out_grad = dot_tn(branch_full, attended[layer].astype(BF16))
        joined = jnp.concatenate(
            [
                query_grad[:, :128],
                query_grad[:, 128:] + out_grad[:, :128],
                out_grad[:, 128:],
            ],
            axis=1,
        )
        grads[layer, :, :, :, QUERY_OUT] = joined.astype(BF16).reshape(4, 4, SHARD, 384)
        partial = dot_nt(grad_query, matrix(layer, QUERY))
        wait_all(waits_a)
        pair_mid_a[layer] = sum_slots(pair_in_a.at[layer]).astype(BF16)
        waits_a = [
            links.exchange(
                "z",
                steps,
                pair_mid_a.at[layer, links.near("z", steps)],
                pair_end_a.at[layer, z],
                pair_end_a.at[layer, links.near("z", -steps)],
            )
            for steps in (2, 1, 3)
        ]
        pair_end_a[layer, z] = pair_mid_a[layer, z]
        wait_all(waits_b)
        pair_mid_b[layer] = sum_slots(pair_in_b.at[layer]).astype(BF16)
        waits_b = [
            links.exchange(
                "x",
                steps,
                pair_mid_b.at[layer, links.near("x", steps)],
                pair_end_b.at[layer, x],
                pair_end_b.at[layer, links.near("x", -steps)],
            )
            for steps in (2, 1, 3)
        ]
        pair_end_b[layer, x] = pair_mid_b[layer, x]
        wait_all(waits_a)
        wait_all(waits_b)
        grad_pair = jnp.concatenate(
            [sum_slots(pair_end_a.at[layer]), sum_slots(pair_end_b.at[layer])], axis=0
        ).astype(BF16)
        partial = partial + dot_nt(grad_pair, matrix(layer, KV))
        waits = scatter_y(links, scatter_out.at[layer, 3], scatter_in.at[layer, 3], partial)
        pair_weight_grad = dot_tn(normed, grad_pair)
        grads[layer, :, :, :, KV] = pair_weight_grad.astype(BF16).reshape(4, 4, SHARD, 384)
        sums[layer, 7:8, :] = jnp.concatenate(
            [
                column_sum(grad_pair.astype(F32)),
                column_sum(grad_query.astype(F32)),
                jnp.zeros((1, 128), F32),
            ],
            axis=1,
        )
        wait_all(waits)
        grad_one = sum_slots(scatter_in.at[layer, 3])
        sums[layer, 0:1, :] = column_sum(grad_one * unit_one)
        sums[layer, 1:2, :] = column_sum(grad_one)
        grad_input = grad_middle + norm_back(grad_one, unit_one, factor_one, gain_one)
        in_grads[layer] = grad_input.astype(BF16)

    backward(1, cotangent[s])
    backward(0, in_grads[1])
    in_grad_wait = links.exchange("s", 1, in_grads.at[other], in_grad_cross, in_grad_cross)

    cross_wait = links.exchange("s", 1, grads.at[other], grads_cross, grads_cross)
    sums_wait = links.exchange("s", 1, sums.at[other], sums_cross, sums_cross)
    sums_wait()
    sums_y[y] = sums[s] + sums_cross[...]
    waits = gather_y(links, sums_y)
    wait_all(waits)
    sums_z[z] = jnp.concatenate([sum_slots(sums_y)[0:6], sums_y[y, 6:8, :]], axis=0)
    z_waits = [
        links.exchange(
            "z", steps, sums_z.at[z], sums_z.at[z], sums_z.at[links.near("z", -steps)]
        )
        for steps in (1, 3, 2)
    ]
    cross_wait()

    def add_cross(step, carry):
        mine = grads[s, step].astype(F32)
        grads[s, step] = (mine + grads_cross[step].astype(F32)).astype(BF16)
        return carry

    lax.fori_loop(0, 4, add_cross, 0)
    waits_a = [
        links.exchange(
            "x",
            steps,
            grads.at[s, links.near("x", steps), :, :, side_a],
            grads_in_a.at[x],
            grads_in_a.at[links.near("x", -steps)],
        )
        for steps in (2, 1, 3)
    ]
    waits_b = [
        links.exchange(
            "z",
            steps,
            grads.at[s, :, links.near("z", steps), :, side_b],
            grads_in_b.at[z],
            grads_in_b.at[links.near("z", -steps)],
        )
        for steps in (2, 1, 3)
    ]
    grads_in_a[x] = grads[s, x, :, :, 0:HALF]
    grads_in_b[z] = grads[s, :, z, :, HALF:COLUMNS]
    wait_all(z_waits)
    sums_x[x] = sum_slots(sums_z)
    x_waits = [
        links.exchange(
            "x", steps, sums_x.at[x], sums_x.at[x], sums_x.at[links.near("x", -steps)]
        )
        for steps in (1, 3, 2)
    ]
    output_wait()
    activations[s] = outputs[s]
    activations[other] = output_cross[...]
    in_grad_wait()
    input_grads[s] = in_grads[s]
    input_grads[other] = in_grad_cross[...]
    wait_all(waits_a)
    grads_mid_a[...] = sum_slots(grads_in_a).astype(BF16)
    waits_a = [
        links.exchange(
            "z",
            steps,
            grads_mid_a.at[links.near("z", steps)],
            grads_end_a.at[z],
            grads_end_a.at[links.near("z", -steps)],
        )
        for steps in (2, 1, 3)
    ]
    grads_end_a[z] = grads_mid_a[z]
    wait_all(waits_b)
    grads_mid_b[...] = sum_slots(grads_in_b).astype(BF16)
    waits_b = [
        links.exchange(
            "x",
            steps,
            grads_mid_b.at[links.near("x", steps)],
            grads_end_b.at[x],
            grads_end_b.at[links.near("x", -steps)],
        )
        for steps in (2, 1, 3)
    ]
    grads_end_b[x] = grads_mid_b[x]
    wait_all(x_waits)
    param_grads[...] = sum_slots(sums_x)
    wait_all(waits_a)
    weight_grads[:, 0:HALF] = sum_slots(grads_end_a)
    wait_all(waits_b)
    weight_grads[:, HALF:COLUMNS] = sum_slots(grads_end_b)
    links.finish()


def scratch_shapes():
    def low(*shape):
        return pltpu.VMEM(shape, BF16)

    def full(*shape):
        return pltpu.VMEM(shape, F32)

    return [
        pltpu.SemaphoreType.DMA((SEMS,)),
        pltpu.SemaphoreType.DMA((SEMS,)),
        low(2, 4, 4, SHARD, COLUMNS),
        full(2, 8, D),
        low(2, 4, ROWS, D),
        low(2, 4, ROWS, D),
        low(2, 4, ROWS, D),
        low(2, 4, ROWS, D),
        low(2, 4, 4, ROWS, D),
        low(2, 4, 4, ROWS, D),
        low(2, 4, 4, FULL, 384),
        full(4, STACK, CHUNK),
        low(2, 4, STACK, CHUNK),
        low(2, STACK, 256),
        full(2, STACK, 1),
        full(2, FULL, 256),
        full(2, ROWS, D),
        full(2, ROWS, D),
        low(2, FULL, D),
        full(2, FULL, D),
        low(2, 4, 4, FULL, 384),
        low(2, 4, 4, 64, 384),
        low(2, 4, 4, 64, 384),
        low(2, 4, 64, 384),
        low(2, 4, 64, 384),
        low(2, 4, 64, 384),
        low(2, 4, 64, 384),
        low(2, 4, 4, SHARD, COLUMNS),
        low(4, 4, SHARD, COLUMNS),
        low(4, 4, SHARD, HALF),
        low(4, 4, SHARD, HALF),
        low(4, SHARD, HALF),
        low(4, SHARD, HALF),
        low(4, SHARD, HALF),
        low(4, SHARD, HALF),
        full(2, 8, D),
        full(8, D),
        full(4, 8, D),
        full(4, 8, D),
        full(4, 8, D),
        low(2, ROWS, D),
        low(ROWS, D),
        low(2, ROWS, D),
        low(ROWS, D),
    ]


def local(
    inputs,
    cotangent,
    ln1_gain,
    ln1_bias,
    w_qkv,
    b_qv,
    w_out,
    b_out,
    ln2_gain,
    ln2_bias,
    w_up,
    b_up,
    w_down,
    b_down,
):
    packed = jnp.concatenate(
        [
            w_up[0],
            w_down[0].T,
            w_qkv[0, :, 1],
            w_qkv[0, :, 2],
            w_qkv[0, :, 0],
            w_out[0].T,
        ],
        axis=1,
    )
    biases = jnp.concatenate(
        [jnp.zeros((1, 192), F32), b_qv[:, 1], b_qv[:, 0], jnp.zeros((1, 192), F32)], axis=1
    )
    params = jnp.concatenate(
        [ln1_gain, ln1_bias, b_out, ln2_gain, ln2_bias, b_down, b_up, biases], axis=0
    )
    whole = pl.BlockSpec(memory_space=pltpu.VMEM)
    acts, in_grads, weight_grads, sums = pl.pallas_call(
        kernel,
        name="layers",
        out_shape=(
            jax.ShapeDtypeStruct((2, ROWS, D), BF16),
            jax.ShapeDtypeStruct((2, ROWS, D), BF16),
            jax.ShapeDtypeStruct((SHARD, COLUMNS), F32),
            jax.ShapeDtypeStruct((8, D), F32),
        ),
        in_specs=[whole] * 4,
        out_specs=(whole,) * 4,
        scratch_shapes=scratch_shapes(),
        compiler_params=pltpu.CompilerParams(
            collective_id=0, has_side_effects=True, vmem_limit_bytes=60 * 2**20
        ),
    )(inputs, cotangent, packed, params)
    qkv_grad = jnp.stack(
        [weight_grads[:, 1920:2112], weight_grads[:, 1536:1728], weight_grads[:, 1728:1920]],
        axis=1,
    )
    return (
        acts[None],
        in_grads[None],
        sums[0:1],
        sums[1:2],
        qkv_grad[None],
        jnp.stack([sums[7, 384:576], sums[7, 192:384]])[None],
        weight_grads[:, 2112:2304].T[None],
        sums[2:3],
        sums[3:4],
        sums[4:5],
        weight_grads[:, UP][None],
        sums[6:7],
        weight_grads[:, DOWN].T[None],
        sums[5:6],
    )


def solution(mesh):
    rows = P(None, ("gx", "gy"), None)
    vector = P("section", None)
    qkv = P("section", "gx", None, "gy")
    bias_qv = P("section", None, "gy")
    out = P("section", "gy", "gx")
    up = P("section", "gx", "gy")
    hidden = P("section", "gy")
    sharded = (vector, vector, qkv, bias_qv, out, vector, vector, vector, up, hidden, out, vector)
    layer_rows = P("section", None, ("gx", "gy"), None)
    return jax.shard_map(
        local,
        mesh=mesh,
        in_specs=(rows, rows) + sharded,
        out_specs=(layer_rows, layer_rows) + sharded,
        check_vma=False,
    )
```

time: 1710 us -> 227 us (0.13); the launches traced: 1690 us -> 226 us
  waiting for transfers between devices: 1220 us -> 0 us
  Pallas kernels: 0 us -> 213 us
  blocking collectives: 199 us -> 0 us
  matrix products: 99 us -> 0 us
  other arithmetic: 82.2 us -> 1.33 us
  local copies, waits for them, and re-layouts: 62.7 us -> 10.5 us
    psum x9 -> x0, waiting for transfers between devices: 461 us -> none  [the longest x3 229 us: local(): lax.psum(jnp.dot(mixed, full_out, preferred_element_type=jnp.float32).ast...]
    all_gather x8 -> x0, waiting for transfers between devices: 296 us -> none  [the longest x3 119 us: local(): lax.all_gather(take_slot(kept_pairs, slot_id), 'gx', axis=0, tiled=True)]
    unnamed x32 -> x0, waiting for transfers between devices: 288 us -> none
    pallas_call x0 -> x1, Pallas kernels: none -> 213 us  [local(): pl.pallas_call(kernel, name='layers', out_shape=(jax.ShapeDtypeStruct((2,...]
    reduce_scatter x5 -> x0, waiting for transfers between devices: 171 us -> none  [the longest x1 70.5 us: local(): lax.psum_scatter(grad_up.astype(jnp.bfloat16), 'gx', scatter_dimension=0,...]
    all_gather x8 -> x0, blocking collectives: 124 us -> none  [the longest x3 37.4 us: local(): grad_full = lax.all_gather(grad_result, 'gy', axis=0, tiled=True)]
    dot_general x63 -> x0, matrix products: 99 us -> none  [the longest x12 18.1 us: block_scores(): jnp.einsum('qhd,khd->hqk', queries, key_block, preferred_element_type=jnp...]
    psum x1 -> x0, blocking collectives: 74.5 us -> none  [local(): lax.psum((gain_one_grad, offset_one_grad, bias_qv_grad, bias_out_grad, ga...]
  transfers between devices with their start and end apart: 31 -> 0, of which waited for: 29 -> 0; matrix products, arithmetic and copies ran while one was open for 8% -> 0% of each run, Pallas kernels for 0% -> 0%
where the time goes in v1:
time: 227 us; the launch traced here: 226 us
  Pallas kernels  213 us (94%)
  local copies, waits for them, and re-layouts  10.5 us (5%)
    pallas_call x1, Pallas kernels, local(): pl.pallas_call(kernel, name='layers', out_shape=(jax.ShapeDtypeStruct((2,...  213 us

profile of v1, /device:TPU:0, one launch (start us, length us, event | category | flops | bytes accessed | tf_op | source)
XLA Modules:
  0.0 225.5 jit_solution(9433472576436597949)
XLA Ops:
  0.6 0.0 copy-start.12
  0.7 0.0 copy-start.11
  0.7 0.0 copy-start.9
  0.7 0.0 copy-start.10
  0.7 0.8 slice_bitcast_fusion.10
  1.5 0.0 copy-start.7
  1.5 0.1 pad_maximum_fusion
  1.5 0.0 copy-done.12
  1.6 0.0 copy-done.11
  1.6 0.0 copy-done.9
  1.6 0.0 copy-done.10
  1.6 0.6 copy-done.8
  2.1 0.0 copy-done.6
  2.1 0.0 copy-done.7
  2.2 0.6 concatenate.11.own_params
  2.8 0.8 slice_bitcast_fusion.6
  3.6 0.0 copy-done.5
  3.6 0.1 copy-done.3
  3.7 0.1 copy-done.4
  3.8 0.8 concatenate.9.own_weights
  4.6 212.9 %layers.1 = (bf16[2,32,768]{2,1,0:T(8,128)(2,1)}, bf16[2,32,768]{2,1,0:T(8,128)(2,1)}, f32[48,2304]{1,0:T(8,128)}, f32[8,768]{1,0:T(8,128)}) custom-call(bf16[2,32,768]{2,1,0:T(8,128)(2,1)} %inputs.1, bf16[2,32,768]{2,1,0:T(8,128)(2,1)} %cotangent.1, bf16[48,2304]{1,0:T(8,128)(2,1)} %concatenate.9.own_weights, f32[8,768]{1,0:T(8,128)} %concatenate.11.own_params), custom_call_target="tpu_custom_call" | custom-call | tf_op jit(solution)/shard_map/layers/pallas_call | solution.py:794
  217.5 0.0 copy-start
  217.5 0.9 fusion.1
  218.4 1.7 fusion
  220.1 0.6 maximum_bitcast_fusion.1
  220.7 1.6 slice_bitcast_fusion.2
  222.3 0.7 slice_bitcast_fusion
  223.0 0.7 maximum_bitcast_fusion
  223.7 0.3 copy-done.2
  223.9 0.6 copy.30
  224.6 0.3 copy-done.1
  224.9 0.6 copy.31
  (9 shorter events, 0.0 us)
Async XLA Ops:
  0.6 0.9 copy-start.12
  0.7 0.9 copy-start.11
  0.7 0.9 copy-start.9
  0.7 0.9 copy-start.10
  1.4 0.7 copy-start.8
  1.5 0.7 copy-start.6
  1.5 0.7 copy-start.7
  2.2 1.5 copy-start.5
  2.8 0.9 copy-start.3
  2.8 1.0 copy-start.4
  217.5 4.8 %copy-start = (f32[48,2304]{1,0:T(8,128)S(1)}, f32[48,2304]{1,0:T(8,128)}, u32[]{:S(2)}) copy-start(f32[48,2304]{1,0:T(8,128)} %get-tuple-element.21) | copy-start | bytes 1327108
  223.0 0.9 copy-start.2
  223.9 0.9 copy-start.1

commit v2 on v1

--- a/solution.py
+++ b/solution.py
@@ -19,16 +19,10 @@
 HEADS = 3
 STACK = HEADS * FULL
 
-UP = slice(0, 768)
-DOWN = slice(768, 1536)
-KV = slice(1536, 1920)
-QUERY = slice(1920, 2176)
-OUT = slice(2048, 2304)
-QUERY_OUT = slice(1920, 2304)
-COLUMNS = 2304
-HALF = COLUMNS // 2
+WIDE = 768
+NARROW = 384
 SHARD = 48
-SEMS = 200
+SEMS = 240
 
 
 def dot_nn(a, b):
@@ -110,8 +104,20 @@
             return 1 - self.section
         return (getattr(self, axis) + (steps + 4)) % 4
 
+    def place(self, first, second):
+        s = self.section
+        x = (self.x + (first + 4) * s + (second + 4) * (1 - s)) % 4
+        z = (self.z + (first + 4) * (1 - s) + (second + 4) * s) % 4
+        return x, z
+
     def device(self, axis, steps):
         s, x, z, y = self.section, self.x, self.z, self.y
+        if axis == "first":
+            x, z = self.place(steps, 0)
+            return (s, x * 4 + z, y)
+        if axis == "second":
+            x, z = self.place(0, steps)
+            return (s, x * 4 + z, y)
         there = self.near(axis, steps)
         if axis == "s":
             s = there
@@ -189,18 +195,113 @@
     return total
 
 
+class Gather:
+    def __init__(self, links, buffer, layer):
+        self.links, self.buffer, self.layer = links, buffer, layer
+
+    def block(self, first, second):
+        x, z = self.links.place(first, second)
+        return self.buffer.at[self.layer, self.links.section, x, z]
+
+    def begin(self):
+        own = self.block(0, 0)
+        exchange = self.links.exchange
+        self.first = [
+            exchange("first", steps, own, own, self.block(-steps, 0)) for steps in (1, 3, 2)
+        ]
+        self.second = [
+            exchange("second", steps, own, own, self.block(0, -steps)) for steps in (1, 3, 2)
+        ]
+
+    def forward(self):
+        for wait, first in zip(self.first, (1, 3, 2)):
+            wait()
+            came = self.block(-first, 0)
+            for steps in (1, 3, 2):
+                self.second.append(
+                    self.links.exchange(
+                        "second", steps, came, came, self.block(-first, -steps)
+                    )
+                )
+
+    def cross(self):
+        wait_all(self.second)
+        s = self.links.section
+        mine = self.buffer.at[self.layer, s]
+        self.finish = self.links.exchange("s", 1, mine, mine, self.buffer.at[self.layer, 1 - s])
+
+
+class Scatter:
+    def __init__(self, links, layer, grads, crossed, work, arrived, middle, ended, done, other):
+        self.links, self.layer, self.grads, self.crossed = links, layer, grads, crossed
+        self.work, self.arrived, self.middle, self.ended = work, arrived, middle, ended
+        self.done, self.other = done.at[layer], other.at[layer]
+        s, x, z = links.section, links.x, links.z
+        self.first_index = z * (1 - s) + x * s
+        self.second_index = x * (1 - s) + z * s
+
+    def begin(self):
+        s = self.links.section
+        self.crossing = self.links.exchange(
+            "s", 1, self.grads.at[self.layer, 1 - s], self.crossed, self.crossed
+        )
+
+    def spread(self, axis, index, source, target):
+        waits = []
+        for steps in (2, 1, 3):
+            waits.append(
+                self.links.exchange(
+                    axis,
+                    steps,
+                    source.at[(index + steps) % 4],
+                    target.at[index],
+                    target.at[(index + 4 - steps) % 4],
+                )
+            )
+        target[index] = source[index]
+        return waits
+
+    def first(self):
+        self.crossing()
+        s = self.links.section
+
+        def add(first, carry):
+            for second in range(4):
+                x = first * s + second * (1 - s)
+                z = first * (1 - s) + second * s
+                mine = self.grads[self.layer, s, x, z].astype(F32)
+                self.work[first, second] = (mine + self.crossed[x, z].astype(F32)).astype(BF16)
+            return carry
+
+        lax.fori_loop(0, 4, add, 0)
+        self.waits = self.spread("first", self.first_index, self.work, self.arrived)
+
+    def second(self):
+        wait_all(self.waits)
+        self.middle[...] = sum_slots(self.arrived).astype(BF16)
+        self.waits = self.spread("second", self.second_index, self.middle, self.ended)
+
+    def last(self):
+        wait_all(self.waits)
+        self.done[...] = sum_slots(self.ended)
+        self.finish = self.links.exchange("s", 1, self.done, self.other, self.other)
+
+
 def kernel(
     inputs,
     cotangent,
-    own_weights,
+    own_wide,
+    own_narrow,
     own_params,
     activations,
     input_grads,
-    weight_grads,
+    wide_out,
+    narrow_out,
     param_grads,
     send_sems,
     recv_sems,
-    weights,
+    wide,
+    narrow,
     params,
     normed_one,
     normed_two,
@@ -225,14 +326,22 @@
     pair_mid_b,
     pair_end_a,
     pair_end_b,
-    grads,
-    grads_cross,
-    grads_in_a,
-    grads_in_b,
-    grads_mid_a,
-    grads_mid_b,
-    grads_end_a,
-    grads_end_b,
+    wide_grads,
+    narrow_grads,
+    wide_crossed,
+    wide_work,
+    wide_arrived,
+    wide_middle,
+    wide_ended,
+    wide_done,
+    wide_other,
+    narrow_crossed,
+    narrow_work,
+    narrow_arrived,
+    narrow_middle,
+    narrow_ended,
+    narrow_done,
+    narrow_other,
     sums,
     sums_cross,
     sums_y,
@@ -246,34 +355,22 @@
     links = Links(send_sems, recv_sems)
     s, x, z, y, row = links.section, links.x, links.z, links.y, links.row
     other = 1 - s
-    side_a, side_b = pl.ds(0, HALF), pl.ds(HALF, HALF)
+    wide[s, :, x, z] = own_wide[...]
+    narrow[s, :, x, z] = own_narrow[...]
+    params[s] = own_params[...]
     links.barrier()
 
-    params[s] = own_params[...]
+    narrow_wait = links.exchange(
+        "s", 1, own_narrow.at[other], narrow.at[s, other, x, z], narrow.at[other, s, x, z]
+    )
     params_wait = links.exchange("s", 1, params.at[s], params.at[s], params.at[other])
-
-    weights[s, x, z] = own_weights[...]
-    first_a = [
-        links.exchange(
-            "z",
-            steps,
-            weights.at[s, x, z, :, side_a],
-            weights.at[s, x, z, :, side_a],
-            weights.at[s, x, links.near("z", -steps), :, side_a],
-        )
-        for steps in (1, 3, 2)
-    ]
-    first_b = [
-        links.exchange(
-            "x",
-            steps,
-            weights.at[s, x, z, :, side_b],
-            weights.at[s, x, z, :, side_b],
-            weights.at[s, links.near("x", -steps), z, :, side_b],
-        )
-        for steps in (1, 3, 2)
-    ]
-
+    wide_wait = links.exchange(
+        "s", 1, own_wide.at[other], wide.at[s, other, x, z], wide.at[other, s, x, z]
+    )
+    narrow_gathers = [Gather(links, narrow, layer) for layer in range(2)]
+    wide_gathers = [Gather(links, wide, layer) for layer in range(2)]
+    narrow_wait()
+    narrow_gathers[0].begin()
     params_wait()
 
     def norm_rows(layer, current):
@@ -284,77 +381,24 @@
 
     normed_waits = norm_rows(0, inputs[s].astype(F32))
 
-    wait_all(first_a)
-    second_a = [
-        links.exchange(
-            "x",
-            steps,
-            weights.at[s, x, :, :, side_a],
-            weights.at[s, x, :, :, side_a],
-            weights.at[s, links.near("x", -steps), :, :, side_a],
-        )
-        for steps in (1, 3, 2)
-    ]
-    wait_all(first_b)
-    second_b = [
-        links.exchange(
-            "z",
-            steps,
-            weights.at[s, :, z, :, side_b],
-            weights.at[s, :, z, :, side_b],
-            weights.at[s, :, links.near("z", -steps), :, side_b],
-        )
-        for steps in (1, 3, 2)
-    ]
-    crossings = [
-        links.exchange(
-            "s",
-            1,
-            weights.at[s, x, :, :, side_a],
-            weights.at[s, x, :, :, side_a],
-            weights.at[other, x, :, :, side_a],
-        ),
-        links.exchange(
-            "s",
-            1,
-            weights.at[s, :, z, :, side_b],
-            weights.at[s, :, z, :, side_b],
-            weights.at[other, :, z, :, side_b],
-        ),
-    ]
-    for index, steps in enumerate((1, 3, 2)):
-        second_a[index]()
-        came = links.near("x", -steps)
-        crossings.append(
-            links.exchange(
-                "s",
-                1,
-                weights.at[s, came, :, :, side_a],
-                weights.at[s, came, :, :, side_a],
-                weights.at[other, came, :, :, side_a],
-            )
-        )
-        second_b[index]()
-        came = links.near("z", -steps)
-        crossings.append(
-            links.exchange(
-                "s",
-                1,
-                weights.at[s, :, came, :, side_b],
-                weights.at[s, :, came, :, side_b],
-                weights.at[other, :, came, :, side_b],
-            )
-        )
-    wait_all(crossings)
-
-    def matrix(layer, columns):
-        width = columns.stop - columns.start
-        return weights[layer, :, :, :, columns].reshape(D, width)
+    wide_wait()
+    narrow_gathers[0].forward()
+    wide_gathers[0].begin()
+    narrow_gathers[0].cross()
+
+    def matrix(buffer, layer, half):
+        return buffer[layer, half].reshape(D, buffer.shape[-1])
+
+    def part(layer, columns):
+        return narrow[layer, 1, :, :, :, columns].reshape(D, 256)
+
+    query_part, out_part = slice(0, 256), slice(128, 384)
 
     def forward(layer, normed_waits):
         wait_all(normed_waits)
+        narrow_gathers[layer].finish()
         normed = normed_one[layer].reshape(FULL, D)
-        pair = dot_nn(normed, matrix(layer, KV)) + params[layer, 7:8, 0:384]
+        pair = dot_nn(normed, matrix(narrow, layer, 0)) + params[layer, 7:8, 0:384]
         pairs[layer, x, z] = pair.astype(BF16)
         own = pairs.at[layer]
         low, high = pl.ds(0, 64), pl.ds(64, 64)
@@ -378,7 +422,7 @@
             )
             for steps in (1, 3, 2)
         ]
-        query = dot_nn(normed, matrix(layer, QUERY)) + params[layer, 7:8, 384:640]
+        query = dot_nn(normed, part(layer, query_part)) + params[layer, 7:8, 384:640]
         query = query.astype(BF16).astype(F32) * 0.125
         queries[layer] = spread_heads(query, 0).astype(BF16)
         wait_all(pair_first_a)
@@ -403,6 +447,10 @@
             )
             for steps in (1, 3, 2)
         ]
+        if layer == 0:
+            wide_gathers[0].forward()
+        else:
+            wide_gathers[1].cross()
         wait_all(pair_second_a)
         wait_all(pair_second_b)
 
@@ -436,27 +484,69 @@
         totals[layer] = total
         attention = join_heads(summed / total, HD)
         attended[layer] = attention
-        partial = dot_nt(attention.astype(BF16), matrix(layer, OUT))
-        wait_all(scatter_y(links, scatter_out.at[layer, 0], scatter_in.at[layer, 0], partial))
+        partial = dot_nt(attention.astype(BF16), part(layer, out_part))
+        waits = scatter_y(links, scatter_out.at[layer, 0], scatter_in.at[layer, 0], partial)
+        if layer == 0:
+            wide_gathers[0].cross()
+            narrow_gathers[1].begin()
+            wide_gathers[1].begin()
+        wait_all(waits)
         middle = hidden[layer] + sum_slots(scatter_in.at[layer, 0]) + params[layer, 2:3, :]
         middles[layer] = middle
         second, _, _ = norm_parts(middle, params[layer, 3:4, :], params[layer, 4:5, :])
         normed_two[layer, y] = second.astype(BF16)
-        wait_all(gather_y(links, normed_two.at[layer]))
+        waits = gather_y(links, normed_two.at[layer])
+        if layer == 0:
+            narrow_gathers[1].forward()
+            wide_gathers[1].forward()
+        wait_all(waits)
+        wide_gathers[layer].finish()
         upward = (
-            dot_nn(normed_two[layer].reshape(FULL, D), matrix(layer, UP)) + params[layer, 6:7, :]
+            dot_nn(normed_two[layer].reshape(FULL, D), matrix(wide, layer, 0)) + params[layer, 6:7, :]
         )
         active, slope = gelu_parts(upward)
         actives[layer] = active.astype(BF16)
         slopes[layer] = slope
-        partial = dot_nt(actives[layer], matrix(layer, DOWN))
-        wait_all(scatter_y(links, scatter_out.at[layer, 1], scatter_in.at[layer, 1], partial))
+        partial = dot_nt(actives[layer], matrix(wide, layer, 1))
+        waits = scatter_y(links, scatter_out.at[layer, 1], scatter_in.at[layer, 1], partial)
+        if layer == 0:
+            narrow_gathers[1].cross()
+        wait_all(waits)
         result = middle + sum_slots(scatter_in.at[layer, 1]) + params[layer, 5:6, :]
         outputs[layer] = result.astype(BF16)
 
     forward(0, normed_waits)
     forward(1, norm_rows(1, outputs[0].astype(F32)))
     output_wait = links.exchange("s", 1, outputs.at[other], output_cross, output_cross)
+
+    def scatters(layer):
+        wide_scatter = Scatter(
+            links,
+            layer,
+            wide_grads,
+            wide_crossed.at[layer],
+            wide_work.at[layer],
+            wide_arrived.at[layer],
+            wide_middle.at[layer],
+            wide_ended.at[layer],
+            wide_done,
+            wide_other,
+        )
+        narrow_scatter = Scatter(
+            links,
+            layer,
+            narrow_grads,
+            narrow_crossed.at[layer],
+            narrow_work.at[layer],
+            narrow_arrived.at[layer],
+            narrow_middle.at[layer],
+            narrow_ended.at[layer],
+            narrow_done,
+            narrow_other,
+        )
+        return wide_scatter, narrow_scatter
+
+    wide_scatters, narrow_scatters = zip(scatters(0), scatters(1))
 
     def backward(layer, grad_rows):
         grad_outs[layer, y] = grad_rows
@@ -465,15 +555,20 @@
         gain_one, gain_two = params[layer, 0:1, :], params[layer, 3:4, :]
         _, unit_one, factor_one = norm_parts(hidden[layer], gain_one, gain_one)
         _, unit_two, factor_two = norm_parts(middles[layer], gain_two, gain_two)
+        if layer == 0:
+            narrow_scatters[1].first()
         wait_all(waits)
         grad_full = grad_outs[layer].reshape(FULL, D)
-        grad_up = (dot_nn(grad_full, matrix(layer, DOWN)) * slopes[layer]).astype(BF16)
-        partial = dot_nt(grad_up, matrix(layer, UP))
+        grad_up = (dot_nn(grad_full, matrix(wide, layer, 1)) * slopes[layer]).astype(BF16)
+        partial = dot_nt(grad_up, matrix(wide, layer, 0))
         waits = scatter_y(links, scatter_out.at[layer, 2], scatter_in.at[layer, 2], partial)
         down_grad = dot_tn(grad_full, actives[layer])
-        grads[layer, :, :, :, DOWN] = down_grad.astype(BF16).reshape(4, 4, SHARD, D)
+        wide_grads[layer, 1] = down_grad.astype(BF16).reshape(4, 4, SHARD, WIDE)
         up_grad = dot_tn(normed_two[layer].reshape(FULL, D), grad_up)
-        grads[layer, :, :, :, UP] = up_grad.astype(BF16).reshape(4, 4, SHARD, D)
+        wide_grads[layer, 0] = up_grad.astype(BF16).reshape(4, 4, SHARD, WIDE)
+        wide_scatters[layer].begin()
+        if layer == 0:
+            narrow_scatters[1].second()
         sums[layer, 6:7, :] = column_sum(grad_up.astype(F32))
         wait_all(waits)
         grad_two = sum_slots(scatter_in.at[layer, 2])
@@ -483,9 +578,10 @@
         sums[layer, 2:3, :] = column_sum(grad_middle)
         sums[layer, 3:4, :] = column_sum(grad_two * unit_two)
         sums[layer, 4:5, :] = column_sum(grad_two)
+        wide_scatters[layer].first()
         wait_all(waits)
         branch_full = grad_branches[layer].reshape(FULL, D)
-        grad_mixed = dot_nn(branch_full, matrix(layer, OUT)).astype(BF16).astype(F32)
+        grad_mixed = dot_nn(branch_full, part(layer, out_part)).astype(BF16).astype(F32)
         stacked_grad = spread_heads(grad_mixed, HD)
         delta = jnp.sum(spread_heads(grad_mixed * attended[layer], HD), axis=1, keepdims=True)
         inverse = 1.0 / totals[layer]
@@ -554,8 +650,11 @@
             ],
             axis=1,
         )
-        grads[layer, :, :, :, QUERY_OUT] = joined.astype(BF16).reshape(4, 4, SHARD, 384)
-        partial = dot_nt(grad_query, matrix(layer, QUERY))
+        narrow_grads[layer, 1] = joined.astype(BF16).reshape(4, 4, SHARD, NARROW)
+        partial = dot_nt(grad_query, part(layer, query_part))
+        wide_scatters[layer].second()
+        if layer == 0:
+            narrow_scatters[1].last()
         wait_all(waits_a)
         pair_mid_a[layer] = sum_slots(pair_in_a.at[layer]).astype(BF16)
         waits_a = [
@@ -587,10 +686,12 @@
         grad_pair = jnp.concatenate(
             [sum_slots(pair_end_a.at[layer]), sum_slots(pair_end_b.at[layer])], axis=0
         ).astype(BF16)
-        partial = partial + dot_nt(grad_pair, matrix(layer, KV))
+        partial = partial + dot_nt(grad_pair, matrix(narrow, layer, 0))
         waits = scatter_y(links, scatter_out.at[layer, 3], scatter_in.at[layer, 3], partial)
         pair_weight_grad = dot_tn(normed, grad_pair)
-        grads[layer, :, :, :, KV] = pair_weight_grad.astype(BF16).reshape(4, 4, SHARD, 384)
+        narrow_grads[layer, 0] = pair_weight_grad.astype(BF16).reshape(4, 4, SHARD, NARROW)
+        narrow_scatters[layer].begin()
+        wide_scatters[layer].last()
         sums[layer, 7:8, :] = jnp.concatenate(
             [
                 column_sum(grad_pair.astype(F32)),
@@ -610,95 +711,44 @@
     backward(0, in_grads[1])
     in_grad_wait = links.exchange("s", 1, in_grads.at[other], in_grad_cross, in_grad_cross)
 
-    cross_wait = links.exchange("s", 1, grads.at[other], grads_cross, grads_cross)
     sums_wait = links.exchange("s", 1, sums.at[other], sums_cross, sums_cross)
+    narrow_scatters[0].first()
     sums_wait()
     sums_y[y] = sums[s] + sums_cross[...]
     waits = gather_y(links, sums_y)
-    wait_all(waits)
-    sums_z[z] = jnp.concatenate([sum_slots(sums_y)[0:6], sums_y[y, 6:8, :]], axis=0)
-    z_waits = [
-        links.exchange(
-            "z", steps, sums_z.at[z], sums_z.at[z], sums_z.at[links.near("z", -steps)]
-        )
-        for steps in (1, 3, 2)
-    ]
-    cross_wait()
-
-    def add_cross(step, carry):
-        mine = grads[s, step].astype(F32)
-        grads[s, step] = (mine + grads_cross[step].astype(F32)).astype(BF16)
-        return carry
-
-    lax.fori_loop(0, 4, add_cross, 0)
-    waits_a = [
-        links.exchange(
-            "x",
-            steps,
-            grads.at[s, links.near("x", steps), :, :, side_a],
-            grads_in_a.at[x],
-            grads_in_a.at[links.near("x", -steps)],
-        )
-        for steps in (2, 1, 3)
-    ]
-    waits_b = [
-        links.exchange(
-            "z",
-            steps,
-            grads.at[s, :, links.near("z", steps), :, side_b],
-            grads_in_b.at[z],
-            grads_in_b.at[links.near("z", -steps)],
-        )
-        for steps in (2, 1, 3)
-    ]
-    grads_in_a[x] = grads[s, x, :, :, 0:HALF]
-    grads_in_b[z] = grads[s, :, z, :, HALF:COLUMNS]
-    wait_all(z_waits)
-    sums_x[x] = sum_slots(sums_z)
-    x_waits = [
-        links.exchange(
-            "x", steps, sums_x.at[x], sums_x.at[x], sums_x.at[links.near("x", -steps)]
-        )
-        for steps in (1, 3, 2)
-    ]
     output_wait()
     activations[s] = outputs[s]
     activations[other] = output_cross[...]
+    wait_all(waits)
+    sums_z[z] = jnp.concatenate([sum_slots(sums_y)[0:6], sums_y[y, 6:8, :]], axis=0)
+    waits = [
+        links.exchange(
+            "z", steps, sums_z.at[z], sums_z.at[z], sums_z.at[links.near("z", -steps)]
+        )
+        for steps in (1, 3, 2)
+    ]
+    narrow_scatters[0].second()
     in_grad_wait()
     input_grads[s] = in_grads[s]
     input_grads[other] = in_grad_cross[...]
-    wait_all(waits_a)
-    grads_mid_a[...] = sum_slots(grads_in_a).astype(BF16)
-    waits_a = [
+    wait_all(waits)
+    sums_x[x] = sum_slots(sums_z)
+    waits = [
         links.exchange(
-            "z",
-            steps,
-            grads_mid_a.at[links.near("z", steps)],
-            grads_end_a.at[z],
-            grads_end_a.at[links.near("z", -steps)],
-        )
-        for steps in (2, 1, 3)
+            "x", steps, sums_x.at[x], sums_x.at[x], sums_x.at[links.near("x", -steps)]
+        )
+        for steps in (1, 3, 2)
     ]
-    grads_end_a[z] = grads_mid_a[z]
-    wait_all(waits_b)
-    grads_mid_b[...] = sum_slots(grads_in_b).astype(BF16)
-    waits_b = [
-        links.exchange(
-            "x",
-            steps,
-            grads_mid_b.at[links.near("x", steps)],
-            grads_end_b.at[x],
-            grads_end_b.at[links.near("x", -steps)],
-        )
-        for steps in (2, 1, 3)
-    ]
-    grads_end_b[x] = grads_mid_b[x]
-    wait_all(x_waits)
+    narrow_scatters[0].last()
+    wait_all(waits)
     param_grads[...] = sum_slots(sums_x)
-    wait_all(waits_a)
-    weight_grads[:, 0:HALF] = sum_slots(grads_end_a)
-    wait_all(waits_b)
-    weight_grads[:, HALF:COLUMNS] = sum_slots(grads_end_b)
+    for layer in range(2):
+        wide_scatters[layer].finish()
+        narrow_scatters[layer].finish()
+    wide_out[s] = wide_done[s]
+    wide_out[other] = wide_other[s]
+    narrow_out[s] = narrow_done[s]
+    narrow_out[other] = narrow_other[s]
     links.finish()
 
 
@@ -712,7 +762,8 @@
     return [
         pltpu.SemaphoreType.DMA((SEMS,)),
         pltpu.SemaphoreType.DMA((SEMS,)),
-        low(2, 4, 4, SHARD, COLUMNS),
+        low(2, 2, 4, 4, SHARD, WIDE),
+        low(2, 2, 4, 4, SHARD, NARROW),
         full(2, 8, D),
         low(2, 4, ROWS, D),
         low(2, 4, ROWS, D),
@@ -737,14 +788,22 @@
         low(2, 4, 64, 384),
         low(2, 4, 64, 384),
         low(2, 4, 64, 384),
-        low(2, 4, 4, SHARD, COLUMNS),
-        low(4, 4, SHARD, COLUMNS),
-        low(4, 4, SHARD, HALF),
-        low(4, 4, SHARD, HALF),
-        low(4, SHARD, HALF),
-        low(4, SHARD, HALF),
-        low(4, SHARD, HALF),
-        low(4, SHARD, HALF),
+        low(2, 2, 4, 4, SHARD, WIDE),
+        low(2, 2, 4, 4, SHARD, NARROW),
+        low(2, 4, 4, SHARD, WIDE),
+        low(2, 4, 4, SHARD, WIDE),
+        low(2, 4, 4, SHARD, WIDE),
+        low(2, 4, SHARD, WIDE),
+        low(2, 4, SHARD, WIDE),
+        full(2, SHARD, WIDE),
+        full(2, SHARD, WIDE),
+        low(2, 4, 4, SHARD, NARROW),
+        low(2, 4, 4, SHARD, NARROW),
+        low(2, 4, 4, SHARD, NARROW),
+        low(2, 4, SHARD, NARROW),
+        low(2, 4, SHARD, NARROW),
+        full(2, SHARD, NARROW),
+        full(2, SHARD, NARROW),
         full(2, 8, D),
         full(8, D),
         full(4, 8, D),
@@ -773,16 +832,12 @@
     w_down,
     b_down,
 ):
-    packed = jnp.concatenate(
+    wide = jnp.stack([w_up[0], w_down[0].T])
+    narrow = jnp.stack(
         [
-            w_up[0],
-            w_down[0].T,
-            w_qkv[0, :, 1],
-            w_qkv[0, :, 2],
-            w_qkv[0, :, 0],
-            w_out[0].T,
-        ],
-        axis=1,
+            jnp.concatenate([w_qkv[0, :, 1], w_qkv[0, :, 2]], axis=1),
+            jnp.concatenate([w_qkv[0, :, 0], w_out[0].T], axis=1),
+        ]
     )
     biases = jnp.concatenate(
         [jnp.zeros((1, 192), F32), b_qv[:, 1], b_qv[:, 0], jnp.zeros((1, 192), F32)], axis=1
@@ -791,24 +846,25 @@
         [ln1_gain, ln1_bias, b_out, ln2_gain, ln2_bias, b_down, b_up, biases], axis=0
     )
     whole = pl.BlockSpec(memory_space=pltpu.VMEM)
-    acts, in_grads, weight_grads, sums = pl.pallas_call(
+    acts, in_grads, wide_grads, narrow_grads, sums = pl.pallas_call(
         kernel,
         name="layers",
         out_shape=(
             jax.ShapeDtypeStruct((2, ROWS, D), BF16),
             jax.ShapeDtypeStruct((2, ROWS, D), BF16),
-            jax.ShapeDtypeStruct((SHARD, COLUMNS), F32),
+            jax.ShapeDtypeStruct((2, SHARD, WIDE), F32),
+            jax.ShapeDtypeStruct((2, SHARD, NARROW), F32),
             jax.ShapeDtypeStruct((8, D), F32),
         ),
-        in_specs=[whole] * 4,
-        out_specs=(whole,) * 4,
+        in_specs=[whole] * 5,
+        out_specs=(whole,) * 5,
         scratch_shapes=scratch_shapes(),
         compiler_params=pltpu.CompilerParams(
             collective_id=0, has_side_effects=True, vmem_limit_bytes=60 * 2**20
         ),
-    )(inputs, cotangent, packed, params)
+    )(inputs, cotangent, wide, narrow, params)
     qkv_grad = jnp.stack(
-        [weight_grads[:, 1920:2112], weight_grads[:, 1536:1728], weight_grads[:, 1728:1920]],
+        [narrow_grads[1, :, :192], narrow_grads[0, :, :192], narrow_grads[0, :, 192:]],
         axis=1,
     )
     return (
@@ -818,13 +874,13 @@
         sums[1:2],
         qkv_grad[None],
         jnp.stack([sums[7, 384:576], sums[7, 192:384]])[None],
-        weight_grads[:, 2112:2304].T[None],
+        narrow_grads[1, :, 192:].T[None],
         sums[2:3],
         sums[3:4],
         sums[4:5],
-        weight_grads[:, UP][None],
+        wide_grads[0][None],
         sums[6:7],
-        weight_grads[:, DOWN].T[None],
+        wide_grads[1].T[None],
         sums[5:6],
     )
 

time: 227 us -> 202 us (0.89)
  Pallas kernels: 213 us -> 187 us
    pallas_call x1, Pallas kernels: 213 us -> 187 us  [local(): pl.pallas_call(kernel, name='layers', out_shape=(jax.ShapeDtypeStruct((2,...]
where the time goes in v2:
time: 202 us; the launch traced here: 201 us
  Pallas kernels  187 us (93%)
  local copies, waits for them, and re-layouts  10.4 us (5%)
  other arithmetic  2.74 us (1%)
    pallas_call x1, Pallas kernels, local(): pl.pallas_call(kernel, name='layers', out_shape=(jax.ShapeDtypeStruct((2,...  187 us

profile of v2, /device:TPU:0, one launch (start us, length us, event | category | flops | bytes accessed | tf_op | source)
XLA Modules:
  0.0 201.3 jit_solution(10541115647324154979)
XLA Ops:
  0.6 0.0 copy-start.11
  0.7 0.0 copy-start.9
  0.7 0.0 copy-start.10
  0.7 0.8 slice_bitcast_fusion.9
  1.4 0.0 copy-start.7
  1.5 0.1 pad_maximum_fusion.2
  1.5 0.0 copy-done.11
  1.5 0.0 copy-done.9
  1.5 0.0 copy-done.10
  1.5 0.6 copy-done.8
  2.1 0.0 copy-done.6
  2.1 0.0 copy-done.7
  2.2 1.3 concatenate.15.own_params
  3.5 0.8 slice_bitcast_fusion.7
  4.3 0.1 maximum_bitcast_fusion.1
  4.4 0.0 copy-start.3
  4.4 0.0 copy-start.4
  4.4 0.6 pad_maximum_fusion.1.own_narrow
  5.0 0.2 copy-done.3
  5.2 0.1 copy-done.4
  5.3 0.7 pad_maximum_fusion.own_wide
  6.0 187.4 %layers.1 = (bf16[2,32,768]{2,1,0:T(8,128)(2,1)}, bf16[2,32,768]{2,1,0:T(8,128)(2,1)}, f32[2,48,768]{2,1,0:T(8,128)}, f32[2,48,384]{2,1,0:T(8,128)}, f32[8,768]{1,0:T(8,128)}) custom-call(bf16[2,32,768]{2,1,0:T(8,128)(2,1)} %inputs.1, bf16[2,32,768]{2,1,0:T(8,128)(2,1)} %cotangent.1, bf16[2,48,768]{2,1,0:T(8,128)(2,1)} %pad_maximum_fusion.own_wide, ...), custom_call_target="tpu_custom_call" | custom-call | tf_op jit(solution)/shard_map/layers/pallas_call | solution.py:849
  193.4 0.9 fusion.1
  194.3 1.6 fusion
  195.9 0.6 maximum_bitcast_fusion.3
  196.5 1.6 slice_bitcast_fusion.1
  198.1 0.7 maximum_bitcast_fusion
  198.8 0.7 slice_bitcast_fusion
  199.5 0.2 copy-done.2
  199.7 0.6 copy.30
  200.3 0.3 copy-done.1
  200.6 0.6 copy.31
  (9 shorter events, 0.0 us)
Async XLA Ops:
  0.6 0.9 copy-start.11
  0.7 0.9 copy-start.9
  0.7 0.9 copy-start.10
  1.4 0.7 copy-start.8
  1.4 0.7 copy-start.6
  1.4 0.7 copy-start.7
  3.5 0.8 copy-start.5
  4.4 0.9 copy-start.3
  4.4 0.9 copy-start.4
  196.5 2.3 %copy-start = (f32[2,48,768]{2,1,0:T(8,128)S(1)}, f32[2,48,768]{2,1,0:T(8,128)}, u32[]{:S(2)}) copy-start(f32[2,48,768]{2,1,0:T(8,128)} %get-tuple-element.23) | copy-start | bytes 884740
  198.8 0.9 copy-start.2
  199.7 0.9 copy-start.1

commit v3 on v2

--- a/solution.py
+++ b/solution.py
@@ -195,9 +195,33 @@
     return total
 
 
+SCHEDULE = {
+    "f0_q": ("w0.begin", "w0.own"),
+    "f0_kv": ("w0.forward",),
+    "f0_rs1": ("w0.relay", "w0.cross", "n1.begin", "n1.own"),
+    "f0_ag2": ("n1.forward", "w1.begin", "w1.own"),
+    "f0_rs2": ("n1.relay", "n1.cross", "w1.forward"),
+    "f1_kv": ("w1.relay",),
+    "f1_rs1": ("w1.cross",),
+    "b1_rs1": ("W1.begin",),
+    "b1_ag2": ("W1.first",),
+    "b1_kv1": ("W1.second",),
+    "b1_rs2": ("N1.begin", "W1.last"),
+    "b0_ag": ("N1.first",),
+    "b0_rs1": ("W0.begin", "N1.second"),
+    "b0_ag2": ("W0.first",),
+    "b0_kv1": ("W0.second", "N1.last"),
+    "b0_rs2": ("N0.begin", "W0.last"),
+}
+RELAYED = ()
+
+
 class Gather:
-    def __init__(self, links, buffer, layer):
+    def __init__(self, links, buffer, layer, relayed):
         self.links, self.buffer, self.layer = links, buffer, layer
+        self.relayed = relayed
+        self.near = []
+        self.far = []
 
     def block(self, first, second):
         x, z = self.links.place(first, second)
@@ -205,27 +229,37 @@
 
     def begin(self):
         own = self.block(0, 0)
-        exchange = self.links.exchange
         self.first = [
-            exchange("first", steps, own, own, self.block(-steps, 0)) for steps in (1, 3, 2)
+            self.links.exchange("first", steps, own, own, self.block(-steps, 0))
+            for steps in (1, 3, 2)
         ]
-        self.second = [
-            exchange("second", steps, own, own, self.block(0, -steps)) for steps in (1, 3, 2)
-        ]
+
+    def send(self, first):
+        came = self.block(-first, 0)
+        for steps in (1, 3) if self.relayed else (1, 3, 2):
+            wait = self.links.exchange("second", steps, came, came, self.block(-first, -steps))
+            (self.near if steps != 2 else self.far).append(wait)
+
+    def own(self):
+        self.send(0)
 
     def forward(self):
         for wait, first in zip(self.first, (1, 3, 2)):
             wait()
-            came = self.block(-first, 0)
-            for steps in (1, 3, 2):
-                self.second.append(
-                    self.links.exchange(
-                        "second", steps, came, came, self.block(-first, -steps)
-                    )
+            self.send(first)
+
+    def relay(self):
+        wait_all(self.near)
+        self.near = []
+        if self.relayed:
+            for first, steps in zip((0, 1, 3, 2), (1, 3, 1, 3)):
+                came = self.block(-first, -steps)
+                self.far.append(
+                    self.links.exchange("second", steps, came, came, self.block(-first, -2))
                 )
 
     def cross(self):
-        wait_all(self.second)
+        wait_all(self.near + self.far)
         s = self.links.section
         mine = self.buffer.at[self.layer, s]
         self.finish = self.links.exchange("s", 1, mine, mine, self.buffer.at[self.layer, 1 - s])
@@ -290,9 +324,18 @@
 def kernel(
     inputs,
     cotangent,
-    own_wide,
-    own_narrow,
-    own_params,
+    ln1_gain,
+    ln1_bias,
+    w_qkv,
+    b_qv,
+    w_out,
+    b_out,
+    ln2_gain,
+    ln2_bias,
+    w_up,
+    b_up,
+    w_down,
+    b_down,
     activations,
     input_grads,
     wide_out,
@@ -300,6 +343,8 @@
     param_grads,
     send_sems,
     recv_sems,
+    own_wide,
+    own_narrow,
     wide,
     narrow,
     params,
@@ -355,9 +400,17 @@
     links = Links(send_sems, recv_sems)
     s, x, z, y, row = links.section, links.x, links.z, links.y, links.row
     other = 1 - s
+    own_wide[0] = w_up[0]
+    own_wide[1] = w_down[0]
+    own_narrow[0] = jnp.concatenate([w_qkv[0, 1], w_qkv[0, 2]], axis=1)
+    own_narrow[1] = jnp.concatenate([w_qkv[0, 0], w_out[0]], axis=1)
+    rows = (ln1_gain, ln1_bias, b_out, ln2_gain, ln2_bias, b_down, b_up)
+    for index, values in enumerate(rows):
+        params[s, index : index + 1, :] = values[...]
+    blank = jnp.zeros((1, 192), F32)
+    params[s, 7:8, :] = jnp.concatenate([blank, b_qv[0, 1:2], b_qv[0, 0:1], blank], axis=1)
     wide[s, :, x, z] = own_wide[...]
     narrow[s, :, x, z] = own_narrow[...]
-    params[s] = own_params[...]
     links.barrier()
 
     narrow_wait = links.exchange(
@@ -367,24 +420,37 @@
     wide_wait = links.exchange(
         "s", 1, own_wide.at[other], wide.at[s, other, x, z], wide.at[other, s, x, z]
     )
-    narrow_gathers = [Gather(links, narrow, layer) for layer in range(2)]
-    wide_gathers = [Gather(links, wide, layer) for layer in range(2)]
+    tasks = {}
+    for layer in range(2):
+        for name, buffer in (("n", narrow), ("w", wide)):
+            name = name + str(layer)
+            tasks[name] = Gather(links, buffer, layer, name in RELAYED)
+
+    def slot(name):
+        for step in SCHEDULE.get(name, ()):
+            task, action = step.split(".")
+            getattr(tasks[task], action)()
+
     narrow_wait()
-    narrow_gathers[0].begin()
+    tasks["n0"].begin()
+    tasks["n0"].own()
     params_wait()
 
     def norm_rows(layer, current):
         hidden[layer] = current
         normed, _, _ = norm_parts(current, params[layer, 0:1, :], params[layer, 1:2, :])
         normed_one[layer, y] = normed.astype(BF16)
-        return gather_y(links, normed_one.at[layer])
+        waits = gather_y(links, normed_one.at[layer])
+        slot(f"f{layer}_ag")
+        return waits
 
     normed_waits = norm_rows(0, inputs[s].astype(F32))
 
     wide_wait()
-    narrow_gathers[0].forward()
-    wide_gathers[0].begin()
-    narrow_gathers[0].cross()
+    tasks["n0"].forward()
+    slot("w")
+    tasks["n0"].relay()
+    tasks["n0"].cross()
 
     def matrix(buffer, layer, half):
         return buffer[layer, half].reshape(D, buffer.shape[-1])
@@ -394,9 +460,13 @@
 
     query_part, out_part = slice(0, 256), slice(128, 384)
 
+    def gather_grads(layer, grad_rows):
+        grad_outs[layer, y] = grad_rows
+        return gather_y(links, grad_outs.at[layer])
+
     def forward(layer, normed_waits):
         wait_all(normed_waits)
-        narrow_gathers[layer].finish()
+        tasks[f"n{layer}"].finish()
         normed = normed_one[layer].reshape(FULL, D)
         pair = dot_nn(normed, matrix(narrow, layer, 0)) + params[layer, 7:8, 0:384]
         pairs[layer, x, z] = pair.astype(BF16)
@@ -425,6 +495,7 @@
         query = dot_nn(normed, part(layer, query_part)) + params[layer, 7:8, 384:640]
         query = query.astype(BF16).astype(F32) * 0.125
         queries[layer] = spread_heads(query, 0).astype(BF16)
+        slot(f"f{layer}_q")
         wait_all(pair_first_a)
         pair_second_a = [
             links.exchange(
@@ -447,10 +518,7 @@
             )
             for steps in (1, 3, 2)
         ]
-        if layer == 0:
-            wide_gathers[0].forward()
-        else:
-            wide_gathers[1].cross()
+        slot(f"f{layer}_kv")
         wait_all(pair_second_a)
         wait_all(pair_second_b)
 
@@ -486,21 +554,16 @@
         attended[layer] = attention
         partial = dot_nt(attention.astype(BF16), part(layer, out_part))
         waits = scatter_y(links, scatter_out.at[layer, 0], scatter_in.at[layer, 0], partial)
-        if layer == 0:
-            wide_gathers[0].cross()
-            narrow_gathers[1].begin()
-            wide_gathers[1].begin()
+        slot(f"f{layer}_rs1")
         wait_all(waits)
         middle = hidden[layer] + sum_slots(scatter_in.at[layer, 0]) + params[layer, 2:3, :]
         middles[layer] = middle
         second, _, _ = norm_parts(middle, params[layer, 3:4, :], params[layer, 4:5, :])
         normed_two[layer, y] = second.astype(BF16)
         waits = gather_y(links, normed_two.at[layer])
-        if layer == 0:
-            narrow_gathers[1].forward()
-            wide_gathers[1].forward()
+        slot(f"f{layer}_ag2")
         wait_all(waits)
-        wide_gathers[layer].finish()
+        tasks[f"w{layer}"].finish()
         upward = (
             dot_nn(normed_two[layer].reshape(FULL, D), matrix(wide, layer, 0)) + params[layer, 6:7, :]
         )
@@ -509,13 +572,13 @@
         slopes[layer] = slope
         partial = dot_nt(actives[layer], matrix(wide, layer, 1))
         waits = scatter_y(links, scatter_out.at[layer, 1], scatter_in.at[layer, 1], partial)
-        if layer == 0:
-            narrow_gathers[1].cross()
+        slot(f"f{layer}_rs2")
         wait_all(waits)
         result = middle + sum_slots(scatter_in.at[layer, 1]) + params[layer, 5:6, :]
         outputs[layer] = result.astype(BF16)
 
     forward(0, normed_waits)
+    cotangent_waits = gather_grads(1, cotangent[s])
     forward(1, norm_rows(1, outputs[0].astype(F32)))
     output_wait = links.exchange("s", 1, outputs.at[other], output_cross, output_cross)
 
@@ -546,17 +609,16 @@
         )
         return wide_scatter, narrow_scatter
 
-    wide_scatters, narrow_scatters = zip(scatters(0), scatters(1))
-
-    def backward(layer, grad_rows):
-        grad_outs[layer, y] = grad_rows
-        waits = gather_y(links, grad_outs.at[layer])
+    for layer in range(2):
+        tasks[f"W{layer}"], tasks[f"N{layer}"] = scatters(layer)
+
+    def backward(layer, waits):
+        grad_rows = grad_outs[layer, y]
         sums[layer, 5:6, :] = column_sum(grad_rows.astype(F32))
         gain_one, gain_two = params[layer, 0:1, :], params[layer, 3:4, :]
         _, unit_one, factor_one = norm_parts(hidden[layer], gain_one, gain_one)
         _, unit_two, factor_two = norm_parts(middles[layer], gain_two, gain_two)
-        if layer == 0:
-            narrow_scatters[1].first()
+        slot(f"b{layer}_ag")
         wait_all(waits)
         grad_full = grad_outs[layer].reshape(FULL, D)
         grad_up = (dot_nn(grad_full, matrix(wide, layer, 1)) * slopes[layer]).astype(BF16)
@@ -566,10 +628,8 @@
         wide_grads[layer, 1] = down_grad.astype(BF16).reshape(4, 4, SHARD, WIDE)
         up_grad = dot_tn(normed_two[layer].reshape(FULL, D), grad_up)
         wide_grads[layer, 0] = up_grad.astype(BF16).reshape(4, 4, SHARD, WIDE)
-        wide_scatters[layer].begin()
-        if layer == 0:
-            narrow_scatters[1].second()
         sums[layer, 6:7, :] = column_sum(grad_up.astype(F32))
+        slot(f"b{layer}_rs1")
         wait_all(waits)
         grad_two = sum_slots(scatter_in.at[layer, 2])
         grad_middle = grad_rows.astype(F32) + norm_back(grad_two, unit_two, factor_two, gain_two)
@@ -578,7 +638,7 @@
         sums[layer, 2:3, :] = column_sum(grad_middle)
         sums[layer, 3:4, :] = column_sum(grad_two * unit_two)
         sums[layer, 4:5, :] = column_sum(grad_two)
-        wide_scatters[layer].first()
+        slot(f"b{layer}_ag2")
         wait_all(waits)
         branch_full = grad_branches[layer].reshape(FULL, D)
         grad_mixed = dot_nn(branch_full, part(layer, out_part)).astype(BF16).astype(F32)
@@ -652,9 +712,7 @@
         )
         narrow_grads[layer, 1] = joined.astype(BF16).reshape(4, 4, SHARD, NARROW)
         partial = dot_nt(grad_query, part(layer, query_part))
-        wide_scatters[layer].second()
-        if layer == 0:
-            narrow_scatters[1].last()
+        slot(f"b{layer}_kv1")
         wait_all(waits_a)
         pair_mid_a[layer] = sum_slots(pair_in_a.at[layer]).astype(BF16)
         waits_a = [
@@ -681,6 +739,7 @@
             for steps in (2, 1, 3)
         ]
         pair_end_b[layer, x] = pair_mid_b[layer, x]
+        slot(f"b{layer}_kv2")
         wait_all(waits_a)
         wait_all(waits_b)
         grad_pair = jnp.concatenate(
@@ -690,8 +749,6 @@
         waits = scatter_y(links, scatter_out.at[layer, 3], scatter_in.at[layer, 3], partial)
         pair_weight_grad = dot_tn(normed, grad_pair)
         narrow_grads[layer, 0] = pair_weight_grad.astype(BF16).reshape(4, 4, SHARD, NARROW)
-        narrow_scatters[layer].begin()
-        wide_scatters[layer].last()
         sums[layer, 7:8, :] = jnp.concatenate(
             [
                 column_sum(grad_pair.astype(F32)),
@@ -700,6 +757,7 @@
             ],
             axis=1,
         )
+        slot(f"b{layer}_rs2")
         wait_all(waits)
         grad_one = sum_slots(scatter_in.at[layer, 3])
         sums[layer, 0:1, :] = column_sum(grad_one * unit_one)
@@ -707,12 +765,12 @@
         grad_input = grad_middle + norm_back(grad_one, unit_one, factor_one, gain_one)
         in_grads[layer] = grad_input.astype(BF16)
 
-    backward(1, cotangent[s])
-    backward(0, in_grads[1])
+    backward(1, cotangent_waits)
+    backward(0, gather_grads(0, in_grads[1]))
     in_grad_wait = links.exchange("s", 1, in_grads.at[other], in_grad_cross, in_grad_cross)
 
     sums_wait = links.exchange("s", 1, sums.at[other], sums_cross, sums_cross)
-    narrow_scatters[0].first()
+    tasks["N0"].first()
     sums_wait()
     sums_y[y] = sums[s] + sums_cross[...]
     waits = gather_y(links, sums_y)
@@ -727,7 +785,7 @@
         )
         for steps in (1, 3, 2)
     ]
-    narrow_scatters[0].second()
+    tasks["N0"].second()
     in_grad_wait()
     input_grads[s] = in_grads[s]
     input_grads[other] = in_grad_cross[...]
@@ -739,12 +797,12 @@
         )
         for steps in (1, 3, 2)
     ]
-    narrow_scatters[0].last()
+    tasks["N0"].last()
     wait_all(waits)
     param_grads[...] = sum_slots(sums_x)
     for layer in range(2):
-        wide_scatters[layer].finish()
-        narrow_scatters[layer].finish()
+        tasks[f"W{layer}"].finish()
+        tasks[f"N{layer}"].finish()
     wide_out[s] = wide_done[s]
     wide_out[other] = wide_other[s]
     narrow_out[s] = narrow_done[s]
@@ -762,6 +820,8 @@
     return [
         pltpu.SemaphoreType.DMA((SEMS,)),
         pltpu.SemaphoreType.DMA((SEMS,)),
+        low(2, SHARD, WIDE),
+        low(2, SHARD, NARROW),
         low(2, 2, 4, 4, SHARD, WIDE),
         low(2, 2, 4, 4, SHARD, NARROW),
         full(2, 8, D),
@@ -816,9 +876,14 @@
     ]
 
 
-def local(
-    inputs,
-    cotangent,
+def result_kernel(
+    acts,
+    in_grads,
+    wide,
+    narrow,
+    sums,
+    activations,
+    input_grads,
     ln1_gain,
     ln1_bias,
     w_qkv,
@@ -832,21 +897,32 @@
     w_down,
     b_down,
 ):
-    wide = jnp.stack([w_up[0], w_down[0].T])
-    narrow = jnp.stack(
-        [
-            jnp.concatenate([w_qkv[0, :, 1], w_qkv[0, :, 2]], axis=1),
-            jnp.concatenate([w_qkv[0, :, 0], w_out[0].T], axis=1),
-        ]
-    )
-    biases = jnp.concatenate(
-        [jnp.zeros((1, 192), F32), b_qv[:, 1], b_qv[:, 0], jnp.zeros((1, 192), F32)], axis=1
-    )
-    params = jnp.concatenate(
-        [ln1_gain, ln1_bias, b_out, ln2_gain, ln2_bias, b_down, b_up, biases], axis=0
-    )
+    activations[0] = acts[...]
+    input_grads[0] = in_grads[...]
+    rows = (ln1_gain, ln1_bias, b_out, ln2_gain, ln2_bias, b_down, b_up)
+    for index, target in enumerate(rows):
+        target[...] = sums[index : index + 1, :]
+    b_qv[0, 0:1, :] = sums[7:8, 384:576]
+    b_qv[0, 1:2, :] = sums[7:8, 192:384]
+    w_up[0] = wide[0]
+    w_down[0] = wide[1]
+    w_qkv[0, 0] = narrow[1, :, :192]
+    w_qkv[0, 1] = narrow[0, :, :192]
+    w_qkv[0, 2] = narrow[0, :, 192:]
+    w_out[0] = narrow[1, :, 192:]
+
+
+def model_rows_first(arrays):
+    arrays = list(arrays)
+    for index in (4, 6, 12):
+        arrays[index] = jnp.swapaxes(arrays[index], 1, 2)
+    return arrays
+
+
+def local(*arrays):
+    arrays = model_rows_first(arrays)
     whole = pl.BlockSpec(memory_space=pltpu.VMEM)
-    acts, in_grads, wide_grads, narrow_grads, sums = pl.pallas_call(
+    results = pl.pallas_call(
         kernel,
         name="layers",
         out_shape=(
@@ -856,33 +932,23 @@
             jax.ShapeDtypeStruct((2, SHARD, NARROW), F32),
             jax.ShapeDtypeStruct((8, D), F32),
         ),
-        in_specs=[whole] * 5,
+        in_specs=[whole] * 14,
         out_specs=(whole,) * 5,
         scratch_shapes=scratch_shapes(),
         compiler_params=pltpu.CompilerParams(
             collective_id=0, has_side_effects=True, vmem_limit_bytes=60 * 2**20
         ),
-    )(inputs, cotangent, wide, narrow, params)
-    qkv_grad = jnp.stack(
-        [narrow_grads[1, :, :192], narrow_grads[0, :, :192], narrow_grads[0, :, 192:]],
-        axis=1,
-    )
-    return (
-        acts[None],
-        in_grads[None],
-        sums[0:1],
-        sums[1:2],
-        qkv_grad[None],
-        jnp.stack([sums[7, 384:576], sums[7, 192:384]])[None],
-        narrow_grads[1, :, 192:].T[None],
-        sums[2:3],
-        sums[3:4],
-        sums[4:5],
-        wide_grads[0][None],
-        sums[6:7],
-        wide_grads[1].T[None],
-        sums[5:6],
-    )
+    )(*arrays)
+    rows = jax.ShapeDtypeStruct((1, 2, ROWS, D), BF16)
+    shapes = [rows, rows] + [jax.ShapeDtypeStruct(a.shape, F32) for a in arrays[2:]]
+    results = pl.pallas_call(
+        result_kernel,
+        name="results",
+        out_shape=shapes,
+        in_specs=[whole] * 5,
+        out_specs=[whole] * 14,
+    )(*results)
+    return tuple(model_rows_first(results))
 
 
 def solution(mesh):

time: 202 us -> 185 us (0.916)
  local copies, waits for them, and re-layouts: 10.4 us -> 0 us
  Pallas kernels: 187 us -> 184 us
  other arithmetic: 2.74 us -> 0 us
    pallas_call x1, Pallas kernels: 187 us -> 182 us  [local(): pl.pallas_call(kernel, name='layers', out_shape=(jax.ShapeDtypeStruct((2,...]
    unnamed x26 -> x0, local copies, waits for them, and re-layouts: 2.68 us -> none
    slice x2 -> x0, local copies, waits for them, and re-layouts: 2.46 us -> none  [the longest x1 1.6 us: local(): sums[5:6]]
    broadcast_in_dim x2 -> x0, local copies, waits for them, and re-layouts: 2.34 us -> none  [the longest x1 1.62 us: local(): narrow_grads[1, :, 192:].T[None]]
    pallas_call x0 -> x1, Pallas kernels: none -> 2.05 us  [local(): pl.pallas_call(result_kernel, name='results', out_shape=shapes, in_specs=...]
where the time goes in v3:
time: 185 us
  Pallas kernels  184 us (99%)
    pallas_call x1, Pallas kernels, local(): pl.pallas_call(kernel, name='layers', out_shape=(jax.ShapeDtypeStruct((2,...  182 us

profile of v3, /device:TPU:0, one launch (start us, length us, event | category | flops | bytes accessed | tf_op | source)
XLA Modules:
  0.0 185.0 jit_solution(17969980903800370668)
XLA Ops:
  0.7 182.1 %layers.1 = (bf16[2,32,768]{2,1,0:T(8,128)(2,1)}, bf16[2,32,768]{2,1,0:T(8,128)(2,1)}, f32[2,48,768]{2,1,0:T(8,128)}, f32[2,48,384]{2,1,0:T(8,128)}, f32[8,768]{1,0:T(8,128)}) custom-call(bf16[2,32,768]{2,1,0:T(8,128)(2,1)} %inputs.1, bf16[2,32,768]{2,1,0:T(8,128)(2,1)} %cotangent.1, f32[1,768]{1,0:T(1,128)} %ln1_gain.1, f32[1,768]{1,0:T(1,128)} %ln1_bias.1, ...), custom_call_target="tpu_custom_call" | custom-call | tf_op jit(solution)/shard_map/layers/pallas_call | solution.py:925
  182.8 2.0 %results.1 = (bf16[1,2,32,768]{3,2,1,0:T(8,128)(2,1)}, bf16[1,2,32,768]{3,2,1,0:T(8,128)(2,1)}, f32[1,768]{1,0:T(1,128)}, f32[1,768]{1,0:T(1,128)}, f32[1,3,48,1...) custom-call(bf16[2,32,768]{2,1,0:T(8,128)(2,1)} %get-tuple-element.3, ...), custom_call_target="tpu_custom_call" | custom-call | tf_op jit(solution)/shard_map/results/pallas_call | solution.py:944

commit v4 on v3

--- a/solution.py
+++ b/solution.py
@@ -20,9 +20,9 @@
 STACK = HEADS * FULL
 
 WIDE = 768
-NARROW = 384
+NARROW = 256
 SHARD = 48
-SEMS = 240
+SEMS = 320
 
 
 def dot_nn(a, b):
@@ -86,6 +86,13 @@
         part = stacked[head * FULL : (head + 1) * FULL]
         total = total + jnp.where(head_mask(head, first), part, 0.0)
     return total
+
+
+def only_if(condition, action):
+    if condition is None:
+        action()
+    else:
+        pl.when(condition)(lambda: action())
 
 
 class Links:
@@ -129,19 +136,19 @@
             y = there
         return (s, x * 4 + z, y)
 
-    def exchange(self, axis, steps, source, target, landing):
+    def exchange(self, axis, steps, source, target, landing, send_if=None, come_if=None):
         index = self.count
         self.count += 1
         sems = (self.send_sems.at[index], self.recv_sems.at[index])
         copy = pltpu.make_async_remote_copy(
             source, target, *sems, device_id=self.device(axis, steps), device_id_type=MESH
         )
-        copy.start()
-        self.sent.append(copy)
+        only_if(send_if, copy.start)
+        self.sent.append((send_if, copy.wait_send))
         arrival = pltpu.make_async_remote_copy(
             landing, landing, *sems, device_id=self.device(axis, -steps), device_id_type=MESH
         )
-        return arrival.wait_recv
+        return lambda: only_if(come_if, arrival.wait_recv)
 
     def barrier(self):
         barrier = pltpu.get_barrier_semaphore()
@@ -153,8 +160,8 @@
         pl.semaphore_wait(barrier, len(peers))
 
     def finish(self):
-        for copy in self.sent:
-            copy.wait_send()
+        for condition, wait in self.sent:
+            only_if(condition, wait)
         self.sent = []
 
 
@@ -196,22 +203,22 @@
 
 
 SCHEDULE = {
-    "f0_q": ("w0.begin", "w0.own"),
-    "f0_kv": ("w0.forward",),
-    "f0_rs1": ("w0.relay", "w0.cross", "n1.begin", "n1.own"),
-    "f0_ag2": ("n1.forward", "w1.begin", "w1.own"),
-    "f0_rs2": ("n1.relay", "n1.cross", "w1.forward"),
-    "f1_kv": ("w1.relay",),
+    "x": ("q0.begin", "q0.own"),
+    "f0_q": ("q0.forward", "w0.begin", "w0.own"),
+    "f0_kv": ("q0.cross", "w0.forward"),
+    "f0_rs1": ("w0.cross", "k1.begin", "k1.own"),
+    "f0_ag2": ("k1.forward", "q1.begin", "q1.own", "w1.begin", "w1.own"),
+    "f0_rs2": ("k1.cross", "q1.forward", "w1.forward"),
+    "f1_q": ("q1.cross",),
     "f1_rs1": ("w1.cross",),
-    "b1_rs1": ("W1.begin",),
-    "b1_ag2": ("W1.first",),
-    "b1_kv1": ("W1.second",),
-    "b1_rs2": ("N1.begin", "W1.last"),
-    "b0_ag": ("N1.first",),
-    "b0_rs1": ("W0.begin", "N1.second"),
-    "b0_ag2": ("W0.first",),
-    "b0_kv1": ("W0.second", "N1.last"),
-    "b0_rs2": ("N0.begin", "W0.last"),
+    "b1_kv1": ("W1.begin", "Q1.begin"),
+    "b1_rs2": ("K1.begin", "W1.first"),
+    "b0_ag": ("Q1.first", "K1.first"),
+    "b0_rs1": ("W0.begin", "W1.second"),
+    "b0_ag2": ("W0.first", "Q1.second", "K1.second"),
+    "b0_kv1": ("Q0.begin",),
+    "b0_kv2": ("W0.second", "Q0.first", "W1.last", "Q1.last", "K1.last"),
+    "b0_rs2": ("K0.begin", "W0.last", "Q0.second"),
 }
 RELAYED = ()
 
@@ -339,17 +346,21 @@
     activations,
     input_grads,
     wide_out,
-    narrow_out,
+    joint_out,
+    side_out,
     param_grads,
     send_sems,
     recv_sems,
     own_wide,
-    own_narrow,
+    own_joint,
+    own_side,
     wide,
-    narrow,
+    joint,
+    side,
     params,
     normed_one,
     normed_two,
+    units,
     grad_outs,
     grad_branches,
     scatter_out,
@@ -358,6 +369,8 @@
     scores,
     probs,
     queries,
+    query_sums,
+    tops,
     totals,
     attended,
     hidden,
@@ -372,7 +385,8 @@
     pair_end_a,
     pair_end_b,
     wide_grads,
-    narrow_grads,
+    joint_grads,
+    side_grads,
     wide_crossed,
     wide_work,
     wide_arrived,
@@ -380,13 +394,20 @@
     wide_ended,
     wide_done,
     wide_other,
-    narrow_crossed,
-    narrow_work,
-    narrow_arrived,
-    narrow_middle,
-    narrow_ended,
-    narrow_done,
-    narrow_other,
+    joint_crossed,
+    joint_work,
+    joint_arrived,
+    joint_middle,
+    joint_ended,
+    joint_done,
+    joint_other,
+    side_crossed,
+    side_work,
+    side_arrived,
+    side_middle,
+    side_ended,
+    side_done,
+    side_other,
     sums,
     sums_cross,
     sums_y,
@@ -402,27 +423,34 @@
     other = 1 - s
     own_wide[0] = w_up[0]
     own_wide[1] = w_down[0]
-    own_narrow[0] = jnp.concatenate([w_qkv[0, 1], w_qkv[0, 2]], axis=1)
-    own_narrow[1] = jnp.concatenate([w_qkv[0, 0], w_out[0]], axis=1)
+    none = jnp.zeros((SHARD, 64), BF16)
+    own_joint[0] = jnp.concatenate([w_qkv[0, 1], none], axis=1)
+    own_joint[1] = jnp.concatenate([none, w_qkv[0, 2]], axis=1)
+    own_side[0] = jnp.concatenate([w_qkv[0, 0], none], axis=1)
+    own_side[1] = jnp.concatenate([none, w_out[0]], axis=1)
     rows = (ln1_gain, ln1_bias, b_out, ln2_gain, ln2_bias, b_down, b_up)
     for index, values in enumerate(rows):
         params[s, index : index + 1, :] = values[...]
     blank = jnp.zeros((1, 192), F32)
     params[s, 7:8, :] = jnp.concatenate([blank, b_qv[0, 1:2], b_qv[0, 0:1], blank], axis=1)
     wide[s, :, x, z] = own_wide[...]
-    narrow[s, :, x, z] = own_narrow[...]
+    joint[s, :, x, z] = own_joint[...]
+    side[s, :, x, z] = own_side[...]
     links.barrier()
 
-    narrow_wait = links.exchange(
-        "s", 1, own_narrow.at[other], narrow.at[s, other, x, z], narrow.at[other, s, x, z]
+    joint_wait = links.exchange(
+        "s", 1, own_joint.at[other], joint.at[s, other, x, z], joint.at[other, s, x, z]
     )
     params_wait = links.exchange("s", 1, params.at[s], params.at[s], params.at[other])
+    side_wait = links.exchange(
+        "s", 1, own_side.at[other], side.at[s, other, x, z], side.at[other, s, x, z]
+    )
     wide_wait = links.exchange(
         "s", 1, own_wide.at[other], wide.at[s, other, x, z], wide.at[other, s, x, z]
     )
     tasks = {}
     for layer in range(2):
-        for name, buffer in (("n", narrow), ("w", wide)):
+        for name, buffer in (("k", joint), ("q", side), ("w", wide)):
             name = name + str(layer)
             tasks[name] = Gather(links, buffer, layer, name in RELAYED)
 
@@ -431,109 +459,113 @@
             task, action = step.split(".")
             getattr(tasks[task], action)()
 
-    narrow_wait()
-    tasks["n0"].begin()
-    tasks["n0"].own()
+    joint_wait()
+    tasks["k0"].begin()
+    tasks["k0"].own()
     params_wait()
 
-    def norm_rows(layer, current):
-        hidden[layer] = current
-        normed, _, _ = norm_parts(current, params[layer, 0:1, :], params[layer, 1:2, :])
-        normed_one[layer, y] = normed.astype(BF16)
-        waits = gather_y(links, normed_one.at[layer])
+    def gather_hidden(layer, current):
+        hidden[layer, y] = current
+        waits = gather_y(links, hidden.at[layer])
         slot(f"f{layer}_ag")
         return waits
 
-    normed_waits = norm_rows(0, inputs[s].astype(F32))
-
+    hidden_waits = gather_hidden(0, inputs[s])
+
+    side_wait()
     wide_wait()
-    tasks["n0"].forward()
+    tasks["k0"].forward()
     slot("w")
-    tasks["n0"].relay()
-    tasks["n0"].cross()
+    tasks["k0"].relay()
+    tasks["k0"].cross()
+    slot("x")
 
     def matrix(buffer, layer, half):
         return buffer[layer, half].reshape(D, buffer.shape[-1])
-
-    def part(layer, columns):
-        return narrow[layer, 1, :, :, :, columns].reshape(D, 256)
-
-    query_part, out_part = slice(0, 256), slice(128, 384)
 
     def gather_grads(layer, grad_rows):
         grad_outs[layer, y] = grad_rows
         return gather_y(links, grad_outs.at[layer])
 
-    def forward(layer, normed_waits):
-        wait_all(normed_waits)
-        tasks[f"n{layer}"].finish()
-        normed = normed_one[layer].reshape(FULL, D)
-        pair = dot_nn(normed, matrix(narrow, layer, 0)) + params[layer, 7:8, 0:384]
+    def forward(layer, hidden_waits):
+        wait_all(hidden_waits)
+        hidden_full = hidden[layer].reshape(FULL, D).astype(F32)
+        normed, unit_rows, _ = norm_parts(hidden_full, params[layer, 0:1, :], params[layer, 1:2, :])
+        normed = normed.astype(BF16)
+        normed_one[layer] = normed
+        units[layer] = unit_rows.reshape(4, ROWS, D)
+        tasks[f"k{layer}"].finish()
+        key = dot_nn(normed, matrix(joint, layer, 0))
+        value = dot_nn(normed, matrix(joint, layer, 1))
+        pair = jnp.concatenate(
+            [key[:, :128], key[:, 128:] + value[:, :128], value[:, 128:]], axis=1
+        )
+        pair = pair + params[layer, 7:8, 0:384]
         pairs[layer, x, z] = pair.astype(BF16)
         own = pairs.at[layer]
         low, high = pl.ds(0, 64), pl.ds(64, 64)
-        pair_first_a = [
-            links.exchange(
-                "z",
-                steps,
-                own.at[x, z, low],
-                own.at[x, z, low],
-                own.at[x, links.near("z", -steps), low],
-            )
-            for steps in (1, 3, 2)
-        ]
-        pair_first_b = [
-            links.exchange(
-                "x",
-                steps,
-                own.at[x, z, high],
-                own.at[x, z, high],
-                own.at[links.near("x", -steps), z, high],
-            )
-            for steps in (1, 3, 2)
-        ]
-        query = dot_nn(normed, part(layer, query_part)) + params[layer, 7:8, 384:640]
+        pair_waits = {steps: [] for steps in range(4)}
+
+        def pairs_x(column, half):
+            for steps in (1, 3, 2):
+                yield steps, links.exchange(
+                    "x",
+                    steps,
+                    own.at[x, column, half],
+                    own.at[x, column, half],
+                    own.at[links.near("x", -steps), column, half],
+                    x <= 3 - steps,
+                    x >= steps,
+                )
+
+        def pairs_z(plane, half, condition):
+            for steps in (1, 3, 2):
+                yield steps, links.exchange(
+                    "z",
+                    steps,
+                    own.at[plane, z, half],
+                    own.at[plane, z, half],
+                    own.at[plane, links.near("z", -steps), half],
+                    condition,
+                    condition,
+                )
+
+        pair_first_a = list(pairs_z(x, low, None))
+        pair_first_b = list(pairs_x(z, high))
+        for steps, wait in pairs_x(z, low):
+            pair_waits[steps].append(wait)
+        pair_waits[0] += [wait for _, wait in pairs_z(x, high, None)]
+        slot(f"f{layer}_q")
+        for (steps_a, wait_a), (steps_b, wait_b) in zip(pair_first_a, pair_first_b):
+            wait_a()
+            for steps, wait in pairs_x(links.near("z", -steps_a), low):
+                pair_waits[steps].append(wait)
+            wait_b()
+            came = links.near("x", -steps_b)
+            pair_waits[steps_b] += [wait for _, wait in pairs_z(came, high, x >= steps_b)]
+        slot(f"f{layer}_kv")
+        tasks[f"q{layer}"].finish()
+        query = dot_nn(normed, matrix(side, layer, 0)) + params[layer, 7:8, 384:640]
         query = query.astype(BF16).astype(F32) * 0.125
         queries[layer] = spread_heads(query, 0).astype(BF16)
-        slot(f"f{layer}_q")
-        wait_all(pair_first_a)
-        pair_second_a = [
-            links.exchange(
-                "x",
-                steps,
-                own.at[x, :, low],
-                own.at[x, :, low],
-                own.at[links.near("x", -steps), :, low],
-            )
-            for steps in (1, 3, 2)
-        ]
-        wait_all(pair_first_b)
-        pair_second_b = [
-            links.exchange(
-                "z",
-                steps,
-                own.at[:, z, high],
-                own.at[:, z, high],
-                own.at[:, links.near("z", -steps), high],
-            )
-            for steps in (1, 3, 2)
-        ]
-        slot(f"f{layer}_kv")
-        wait_all(pair_second_a)
-        wait_all(pair_second_b)
 
         stacked = queries[layer]
         position = lax.broadcasted_iota(jnp.int32, (STACK, CHUNK), 0) % FULL + row * FULL
         column = lax.broadcasted_iota(jnp.int32, (STACK, CHUNK), 1)
 
-        def find_top(chunk, running):
+        def find_top(chunk):
             keys = pairs[layer, chunk, :, :, 0:256].reshape(CHUNK, 256)
             raw = dot_nt(stacked, keys)
             raw = jnp.where(column + chunk * CHUNK <= position, raw, MASKED)
             scores[chunk] = raw
-            return jnp.maximum(running, jnp.max(raw, axis=1, keepdims=True))
-
-        top = lax.fori_loop(0, x + 1, find_top, jnp.full((STACK, 1), MASKED, F32))
+            tops[...] = jnp.maximum(tops[...], jnp.max(raw, axis=1, keepdims=True))
+
+        tops[...] = jnp.full((STACK, 1), MASKED, F32)
+        for steps in (0, 1, 3, 2):
+            wait_all(pair_waits[steps])
+            chunk = links.near("x", -steps)
+            only_if(None if steps == 0 else x >= steps, lambda: find_top(chunk))
+        top = tops[...]
 
         def add_chunk(chunk, carry):
             total, summed = carry
@@ -552,12 +584,13 @@
         totals[layer] = total
         attention = join_heads(summed / total, HD)
         attended[layer] = attention
-        partial = dot_nt(attention.astype(BF16), part(layer, out_part))
+        partial = dot_nt(attention.astype(BF16), matrix(side, layer, 1))
         waits = scatter_y(links, scatter_out.at[layer, 0], scatter_in.at[layer, 0], partial)
         slot(f"f{layer}_rs1")
         wait_all(waits)
-        middle = hidden[layer] + sum_slots(scatter_in.at[layer, 0]) + params[layer, 2:3, :]
-        middles[layer] = middle
+        middle = hidden[layer, y].astype(F32) + sum_slots(scatter_in.at[layer, 0])
+        middle = middle + params[layer, 2:3, :]
+        middles[layer, y] = middle
         second, _, _ = norm_parts(middle, params[layer, 3:4, :], params[layer, 4:5, :])
         normed_two[layer, y] = second.astype(BF16)
         waits = gather_y(links, normed_two.at[layer])
@@ -574,12 +607,12 @@
         waits = scatter_y(links, scatter_out.at[layer, 1], scatter_in.at[layer, 1], partial)
         slot(f"f{layer}_rs2")
         wait_all(waits)
-        result = middle + sum_slots(scatter_in.at[layer, 1]) + params[layer, 5:6, :]
+        result = middles[layer, y] + sum_slots(scatter_in.at[layer, 1]) + params[layer, 5:6, :]
         outputs[layer] = result.astype(BF16)
 
-    forward(0, normed_waits)
+    forward(0, hidden_waits)
     cotangent_waits = gather_grads(1, cotangent[s])
-    forward(1, norm_rows(1, outputs[0].astype(F32)))
+    forward(1, gather_hidden(1, outputs[0]))
     output_wait = links.exchange("s", 1, outputs.at[other], output_cross, output_cross)
 
     def scatters(layer):
@@ -595,29 +628,43 @@
             wide_done,
             wide_other,
         )
-        narrow_scatter = Scatter(
+        joint_scatter = Scatter(
             links,
             layer,
-            narrow_grads,
-            narrow_crossed.at[layer],
-            narrow_work.at[layer],
-            narrow_arrived.at[layer],
-            narrow_middle.at[layer],
-            narrow_ended.at[layer],
-            narrow_done,
-            narrow_other,
-        )
-        return wide_scatter, narrow_scatter
+            joint_grads,
+            joint_crossed.at[layer],
+            joint_work.at[layer],
+            joint_arrived.at[layer],
+            joint_middle.at[layer],
+            joint_ended.at[layer],
+            joint_done,
+            joint_other,
+        )
+        side_scatter = Scatter(
+            links,
+            layer,
+            side_grads,
+            side_crossed.at[layer],
+            side_work.at[layer],
+            side_arrived.at[layer],
+            side_middle.at[layer],
+            side_ended.at[layer],
+            side_done,
+            side_other,
+        )
+        return wide_scatter, joint_scatter, side_scatter
 
     for layer in range(2):
-        tasks[f"W{layer}"], tasks[f"N{layer}"] = scatters(layer)
+        tasks[f"W{layer}"], tasks[f"K{layer}"], tasks[f"Q{layer}"] = scatters(layer)
+
+    sum_waits = []
 
     def backward(layer, waits):
         grad_rows = grad_outs[layer, y]
         sums[layer, 5:6, :] = column_sum(grad_rows.astype(F32))
         gain_one, gain_two = params[layer, 0:1, :], params[layer, 3:4, :]
-        _, unit_one, factor_one = norm_parts(hidden[layer], gain_one, gain_one)
-        _, unit_two, factor_two = norm_parts(middles[layer], gain_two, gain_two)
+        _, unit_one, factor_one = norm_parts(hidden[layer, y].astype(F32), gain_one, gain_one)
+        _, unit_two, factor_two = norm_parts(middles[layer, y], gain_two, gain_two)
         slot(f"b{layer}_ag")
         wait_all(waits)
         grad_full = grad_outs[layer].reshape(FULL, D)
@@ -641,7 +688,7 @@
         slot(f"b{layer}_ag2")
         wait_all(waits)
         branch_full = grad_branches[layer].reshape(FULL, D)
-        grad_mixed = dot_nn(branch_full, part(layer, out_part)).astype(BF16).astype(F32)
+        grad_mixed = dot_nn(branch_full, matrix(side, layer, 1)).astype(BF16).astype(F32)
         stacked_grad = spread_heads(grad_mixed, HD)
         delta = jnp.sum(spread_heads(grad_mixed * attended[layer], HD), axis=1, keepdims=True)
         inverse = 1.0 / totals[layer]
@@ -649,7 +696,11 @@
         stacked_grad = stacked_grad.astype(BF16)
         stacked = queries[layer]
 
-        def chunk_back(chunk, summed):
+        own = pair_grads.at[layer]
+        low, high = pl.ds(0, 64), pl.ds(64, 64)
+        waits_a, waits_b = [], []
+
+        def chunk_back(chunk):
             keys = pairs[layer, chunk, :, :, 0:256].reshape(CHUNK, 256)
             values = pairs[layer, chunk, :, :, 128:384].reshape(CHUNK, 256)
             weight = probs[layer, chunk]
@@ -666,52 +717,55 @@
                 axis=1,
             )
             pair_grads[layer, chunk] = joined.astype(BF16).reshape(4, FULL, 384)
-            return summed + dot_nn(score_grad, keys)
-
-        def chunk_clear(chunk, carry):
-            pair_grads[layer, chunk] = jnp.zeros((4, FULL, 384), BF16)
-            return carry
-
-        lax.fori_loop(x + 1, 4, chunk_clear, 0)
-        query_sum = lax.fori_loop(0, x + 1, chunk_back, jnp.zeros((STACK, 256), F32))
-        own = pair_grads.at[layer]
-        low, high = pl.ds(0, 64), pl.ds(64, 64)
-        waits_a = [
-            links.exchange(
-                "x",
-                steps,
-                own.at[links.near("x", steps), :, low],
-                pair_in_a.at[layer, x],
-                pair_in_a.at[layer, links.near("x", -steps)],
+            pair_in_b[layer, z, chunk] = pair_grads[layer, chunk, z, 64:128]
+            query_sums[...] = query_sums[...] + dot_nn(score_grad, keys)
+
+        def earlier(chunk):
+            chunk_back(chunk)
+            pair_in_a[layer, chunk] = jnp.zeros((4, 64, 384), BF16)
+            pair_end_b[layer, chunk] = jnp.zeros((64, 384), BF16)
+
+        def send_z(chunk, condition):
+            for steps in (2, 1, 3):
+                waits_b.append(
+                    links.exchange(
+                        "z",
+                        steps,
+                        own.at[chunk, links.near("z", steps), high],
+                        pair_in_b.at[layer, z, chunk],
+                        pair_in_b.at[layer, links.near("z", -steps), chunk],
+                        condition,
+                        condition,
+                    )
+                )
+
+        query_sums[...] = jnp.zeros((STACK, 256), F32)
+        for steps in (3, 2, 1):
+            chunk = links.near("x", -steps)
+            pl.when(x >= steps)(lambda: earlier(chunk))
+            waits_a.append(
+                links.exchange(
+                    "x",
+                    -steps,
+                    own.at[chunk, :, low],
+                    pair_in_a.at[layer, x],
+                    pair_in_a.at[layer, links.near("x", steps)],
+                    x >= steps,
+                    x <= 3 - steps,
+                )
             )
-            for steps in (2, 1, 3)
-        ]
-        waits_b = [
-            links.exchange(
-                "z",
-                steps,
-                own.at[:, links.near("z", steps), high],
-                pair_in_b.at[layer, z],
-                pair_in_b.at[layer, links.near("z", -steps)],
-            )
-            for steps in (2, 1, 3)
-        ]
+            send_z(chunk, x >= steps)
+        chunk_back(x)
+        send_z(x, None)
         pair_in_a[layer, x] = pair_grads[layer, x, :, 0:64]
-        pair_in_b[layer, z] = pair_grads[layer, :, z, 64:128]
+        query_sum = query_sums[...]
         grad_query = (join_heads(query_sum, 0) * 0.125).astype(BF16)
-        normed = normed_one[layer].reshape(FULL, D)
+        normed = normed_one[layer]
         query_grad = dot_tn(normed, grad_query)
+        side_grads[layer, 0] = query_grad.astype(BF16).reshape(4, 4, SHARD, NARROW)
         out_grad = dot_tn(branch_full, attended[layer].astype(BF16))
-        joined = jnp.concatenate(
-            [
-                query_grad[:, :128],
-                query_grad[:, 128:] + out_grad[:, :128],
-                out_grad[:, 128:],
-            ],
-            axis=1,
-        )
-        narrow_grads[layer, 1] = joined.astype(BF16).reshape(4, 4, SHARD, NARROW)
-        partial = dot_nt(grad_query, part(layer, query_part))
+        side_grads[layer, 1] = out_grad.astype(BF16).reshape(4, 4, SHARD, NARROW)
+        partial = dot_nt(grad_query, matrix(side, layer, 0))
         slot(f"b{layer}_kv1")
         wait_all(waits_a)
         pair_mid_a[layer] = sum_slots(pair_in_a.at[layer]).astype(BF16)
@@ -727,17 +781,26 @@
         ]
         pair_end_a[layer, z] = pair_mid_a[layer, z]
         wait_all(waits_b)
-        pair_mid_b[layer] = sum_slots(pair_in_b.at[layer]).astype(BF16)
-        waits_b = [
-            links.exchange(
-                "x",
-                steps,
-                pair_mid_b.at[layer, links.near("x", steps)],
-                pair_end_b.at[layer, x],
-                pair_end_b.at[layer, links.near("x", -steps)],
+
+        def sum_chunk(chunk):
+            pair_mid_b[layer, chunk] = sum_slots(pair_in_b.at[layer, :, chunk]).astype(BF16)
+
+        waits_b = []
+        for steps in (3, 2, 1):
+            chunk = links.near("x", -steps)
+            pl.when(x >= steps)(lambda: sum_chunk(chunk))
+            waits_b.append(
+                links.exchange(
+                    "x",
+                    -steps,
+                    pair_mid_b.at[layer, chunk],
+                    pair_end_b.at[layer, x],
+                    pair_end_b.at[layer, links.near("x", steps)],
+                    x >= steps,
+                    x <= 3 - steps,
+                )
             )
-            for steps in (2, 1, 3)
-        ]
+        sum_chunk(x)
         pair_end_b[layer, x] = pair_mid_b[layer, x]
         slot(f"b{layer}_kv2")
         wait_all(waits_a)
@@ -745,10 +808,15 @@
         grad_pair = jnp.concatenate(
             [sum_slots(pair_end_a.at[layer]), sum_slots(pair_end_b.at[layer])], axis=0
         ).astype(BF16)
-        partial = partial + dot_nt(grad_pair, matrix(narrow, layer, 0))
+        partial = partial + dot_nt(grad_pair[:, 0:256], matrix(joint, layer, 0))
+        partial = partial + dot_nt(grad_pair[:, 128:384], matrix(joint, layer, 1))
         waits = scatter_y(links, scatter_out.at[layer, 3], scatter_in.at[layer, 3], partial)
-        pair_weight_grad = dot_tn(normed, grad_pair)
-        narrow_grads[layer, 0] = pair_weight_grad.astype(BF16).reshape(4, 4, SHARD, NARROW)
+        key_weight_grad = dot_tn(normed, grad_pair[:, 0:256])
+        joint_grads[layer, 0] = key_weight_grad.astype(BF16).reshape(4, 4, SHARD, NARROW)
+        value_weight_grad = dot_tn(normed, grad_pair[:, 128:384])
+        joint_grads[layer, 1] = value_weight_grad.astype(BF16).reshape(4, 4, SHARD, NARROW)
+        sums[layer, 0:1, :] = column_sum(partial * units[layer].reshape(FULL, D))
+        sums[layer, 1:2, :] = column_sum(partial)
         sums[layer, 7:8, :] = jnp.concatenate(
             [
                 column_sum(grad_pair.astype(F32)),
@@ -758,10 +826,13 @@
             axis=1,
         )
         slot(f"b{layer}_rs2")
+        if layer == 0:
+            sums_wait = links.exchange("s", 1, sums.at[other], sums_cross, sums_cross)
+            sums_wait()
+            sums_y[y] = sums[s] + sums_cross[...]
+            sum_waits.extend(gather_y(links, sums_y))
         wait_all(waits)
         grad_one = sum_slots(scatter_in.at[layer, 3])
-        sums[layer, 0:1, :] = column_sum(grad_one * unit_one)
-        sums[layer, 1:2, :] = column_sum(grad_one)
         grad_input = grad_middle + norm_back(grad_one, unit_one, factor_one, gain_one)
         in_grads[layer] = grad_input.astype(BF16)
 
@@ -769,15 +840,11 @@
     backward(0, gather_grads(0, in_grads[1]))
     in_grad_wait = links.exchange("s", 1, in_grads.at[other], in_grad_cross, in_grad_cross)
 
-    sums_wait = links.exchange("s", 1, sums.at[other], sums_cross, sums_cross)
-    tasks["N0"].first()
-    sums_wait()
-    sums_y[y] = sums[s] + sums_cross[...]
-    waits = gather_y(links, sums_y)
+    tasks["K0"].first()
     output_wait()
     activations[s] = outputs[s]
     activations[other] = output_cross[...]
-    wait_all(waits)
+    wait_all(sum_waits)
     sums_z[z] = jnp.concatenate([sum_slots(sums_y)[0:6], sums_y[y, 6:8, :]], axis=0)
     waits = [
         links.exchange(
@@ -785,7 +852,8 @@
         )
         for steps in (1, 3, 2)
     ]
-    tasks["N0"].second()
+    tasks["Q0"].last()
+    tasks["K0"].second()
     in_grad_wait()
     input_grads[s] = in_grads[s]
     input_grads[other] = in_grad_cross[...]
@@ -797,16 +865,19 @@
         )
         for steps in (1, 3, 2)
     ]
-    tasks["N0"].last()
+    tasks["K0"].last()
     wait_all(waits)
     param_grads[...] = sum_slots(sums_x)
     for layer in range(2):
         tasks[f"W{layer}"].finish()
-        tasks[f"N{layer}"].finish()
+        tasks[f"K{layer}"].finish()
+        tasks[f"Q{layer}"].finish()
     wide_out[s] = wide_done[s]
     wide_out[other] = wide_other[s]
-    narrow_out[s] = narrow_done[s]
-    narrow_out[other] = narrow_other[s]
+    joint_out[s] = joint_done[s]
+    joint_out[other] = joint_other[s]
+    side_out[s] = side_done[s]
+    side_out[other] = side_other[s]
     links.finish()
 
 
@@ -822,11 +893,14 @@
         pltpu.SemaphoreType.DMA((SEMS,)),
         low(2, SHARD, WIDE),
         low(2, SHARD, NARROW),
+        low(2, SHARD, NARROW),
         low(2, 2, 4, 4, SHARD, WIDE),
         low(2, 2, 4, 4, SHARD, NARROW),
+        low(2, 2, 4, 4, SHARD, NARROW),
         full(2, 8, D),
+        low(2, FULL, D),
         low(2, 4, ROWS, D),
-        low(2, 4, ROWS, D),
+        full(2, 4, ROWS, D),
         low(2, 4, ROWS, D),
         low(2, 4, ROWS, D),
         low(2, 4, 4, ROWS, D),
@@ -835,10 +909,12 @@
         full(4, STACK, CHUNK),
         low(2, 4, STACK, CHUNK),
         low(2, STACK, 256),
+        full(STACK, 256),
+        full(STACK, 1),
         full(2, STACK, 1),
         full(2, FULL, 256),
-        full(2, ROWS, D),
-        full(2, ROWS, D),
+        low(2, 4, ROWS, D),
+        full(2, 4, ROWS, D),
         low(2, FULL, D),
         full(2, FULL, D),
         low(2, 4, 4, FULL, 384),
@@ -850,6 +926,7 @@
         low(2, 4, 64, 384),
         low(2, 2, 4, 4, SHARD, WIDE),
         low(2, 2, 4, 4, SHARD, NARROW),
+        low(2, 2, 4, 4, SHARD, NARROW),
         low(2, 4, 4, SHARD, WIDE),
         low(2, 4, 4, SHARD, WIDE),
         low(2, 4, 4, SHARD, WIDE),
@@ -857,6 +934,13 @@
         low(2, 4, SHARD, WIDE),
         full(2, SHARD, WIDE),
         full(2, SHARD, WIDE),
+        low(2, 4, 4, SHARD, NARROW),
+        low(2, 4, 4, SHARD, NARROW),
+        low(2, 4, 4, SHARD, NARROW),
+        low(2, 4, SHARD, NARROW),
+        low(2, 4, SHARD, NARROW),
+        full(2, SHARD, NARROW),
+        full(2, SHARD, NARROW),
         low(2, 4, 4, SHARD, NARROW),
         low(2, 4, 4, SHARD, NARROW),
         low(2, 4, 4, SHARD, NARROW),
@@ -880,7 +964,8 @@
     acts,
     in_grads,
     wide,
-    narrow,
+    joint,
+    side,
     sums,
     activations,
     input_grads,
@@ -906,10 +991,10 @@
     b_qv[0, 1:2, :] = sums[7:8, 192:384]
     w_up[0] = wide[0]
     w_down[0] = wide[1]
-    w_qkv[0, 0] = narrow[1, :, :192]
-    w_qkv[0, 1] = narrow[0, :, :192]
-    w_qkv[0, 2] = narrow[0, :, 192:]
-    w_out[0] = narrow[1, :, 192:]
+    w_qkv[0, 0] = side[0, :, :192]
+    w_qkv[0, 1] = joint[0, :, :192]
+    w_qkv[0, 2] = joint[1, :, 64:]
+    w_out[0] = side[1, :, 64:]
 
 
 def model_rows_first(arrays):
@@ -930,10 +1015,11 @@
             jax.ShapeDtypeStruct((2, ROWS, D), BF16),
             jax.ShapeDtypeStruct((2, SHARD, WIDE), F32),
             jax.ShapeDtypeStruct((2, SHARD, NARROW), F32),
+            jax.ShapeDtypeStruct((2, SHARD, NARROW), F32),
             jax.ShapeDtypeStruct((8, D), F32),
         ),
         in_specs=[whole] * 14,
-        out_specs=(whole,) * 5,
+        out_specs=(whole,) * 6,
         scratch_shapes=scratch_shapes(),
         compiler_params=pltpu.CompilerParams(
             collective_id=0, has_side_effects=True, vmem_limit_bytes=60 * 2**20
@@ -945,7 +1031,7 @@
         result_kernel,
         name="results",
         out_shape=shapes,
-        in_specs=[whole] * 5,
+        in_specs=[whole] * 6,
         out_specs=[whole] * 14,
     )(*results)
     return tuple(model_rows_first(results))

time: 185 us -> 174 us (0.941)
  Pallas kernels: 184 us -> 172 us
    pallas_call x1, Pallas kernels: 182 us -> 170 us  [local(): pl.pallas_call(kernel, name='layers', out_shape=(jax.ShapeDtypeStruct((2,...]
where the time goes in v4:
time: 174 us; the launch traced here: 173 us
  Pallas kernels  172 us (99%)
    pallas_call x1, Pallas kernels, local(): pl.pallas_call(kernel, name='layers', out_shape=(jax.ShapeDtypeStruct((2,...  170 us

profile of v4, /device:TPU:0, one launch (start us, length us, event | category | flops | bytes accessed | tf_op | source)
XLA Modules:
  0.0 173.2 jit_solution(5880241969743299869)
XLA Ops:
  0.7 170.3 %layers.1 = (bf16[2,32,768]{2,1,0:T(8,128)(2,1)}, bf16[2,32,768]{2,1,0:T(8,128)(2,1)}, f32[2,48,768]{2,1,0:T(8,128)}, f32[2,48,256]{2,1,0:T(8,128)}, f32[2,48,256]{2,1,0:T(8,128)}, /*index=5*/f32[8,768]{1,0:T(8,128)}) custom-call(bf16[2,32,768]{2,1,0:T(8,128)(2,1)} %inputs.1, bf16[2,32,768]{2,1,0:T(8,128)(2,1)} %cotangent.1, f32[1,768]{1,0:T(1,128)} %ln1_gain.1, ...), custom_call_target="tpu_custom_call" | custom-call | tf_op jit(solution)/shard_map/layers/pallas_call | solution.py:1010
  171.0 2.0 %results.1 = (bf16[1,2,32,768]{3,2,1,0:T(8,128)(2,1)}, bf16[1,2,32,768]{3,2,1,0:T(8,128)(2,1)}, f32[1,768]{1,0:T(1,128)}, f32[1,768]{1,0:T(1,128)}, f32[1,3,48,1...) custom-call(bf16[2,32,768]{2,1,0:T(8,128)(2,1)} %get-tuple-element.3, ...), custom_call_target="tpu_custom_call" | custom-call | tf_op jit(solution)/shard_map/results/pallas_call | solution.py:1030

commit v5 on v4

--- a/solution.py
+++ b/solution.py
@@ -23,6 +23,8 @@
 NARROW = 256
 SHARD = 48
 SEMS = 320
+PAIR_STEPS = (1, 3, 2)
+GATHER_STEPS = (1, 3, 2)
 
 
 def dot_nn(a, b):
@@ -174,7 +176,7 @@
     y = links.y
     return [
         links.exchange("y", steps, buffer.at[y], buffer.at[y], buffer.at[links.near("y", -steps)])
-        for steps in (1, 3, 2)
+        for steps in GATHER_STEPS
     ]
 
 
@@ -218,7 +220,7 @@
     "b0_ag2": ("W0.first", "Q1.second", "K1.second"),
     "b0_kv1": ("Q0.begin",),
     "b0_kv2": ("W0.second", "Q0.first", "W1.last", "Q1.last", "K1.last"),
-    "b0_rs2": ("K0.begin", "W0.last", "Q0.second"),
+    "b0_rs2": ("W0.last", "Q0.second"),
 }
 RELAYED = ()
 
@@ -487,6 +489,8 @@
         grad_outs[layer, y] = grad_rows
         return gather_y(links, grad_outs.at[layer])
 
+    cotangent_waits = []
+
     def forward(layer, hidden_waits):
         wait_all(hidden_waits)
         hidden_full = hidden[layer].reshape(FULL, D).astype(F32)
@@ -507,7 +511,7 @@
         pair_waits = {steps: [] for steps in range(4)}
 
         def pairs_x(column, half):
-            for steps in (1, 3, 2):
+            for steps in PAIR_STEPS:
                 yield steps, links.exchange(
                     "x",
                     steps,
@@ -543,6 +547,8 @@
             wait_b()
             came = links.near("x", -steps_b)
             pair_waits[steps_b] += [wait for _, wait in pairs_z(came, high, x >= steps_b)]
+        if layer == 0:
+            cotangent_waits.extend(gather_grads(1, cotangent[s]))
         slot(f"f{layer}_kv")
         tasks[f"q{layer}"].finish()
         query = dot_nn(normed, matrix(side, layer, 0)) + params[layer, 7:8, 384:640]
@@ -611,7 +617,6 @@
         outputs[layer] = result.astype(BF16)
 
     forward(0, hidden_waits)
-    cotangent_waits = gather_grads(1, cotangent[s])
     forward(1, gather_hidden(1, outputs[0]))
     output_wait = links.exchange("s", 1, outputs.at[other], output_cross, output_cross)
 
@@ -808,13 +813,20 @@
         grad_pair = jnp.concatenate(
             [sum_slots(pair_end_a.at[layer]), sum_slots(pair_end_b.at[layer])], axis=0
         ).astype(BF16)
+        def joint_gradients():
+            key_weight_grad = dot_tn(normed, grad_pair[:, 0:256])
+            joint_grads[layer, 0] = key_weight_grad.astype(BF16).reshape(4, 4, SHARD, NARROW)
+            value_weight_grad = dot_tn(normed, grad_pair[:, 128:384])
+            joint_grads[layer, 1] = value_weight_grad.astype(BF16).reshape(4, 4, SHARD, NARROW)
+
+        if layer == 0:
+            joint_gradients()
+            tasks["K0"].begin()
         partial = partial + dot_nt(grad_pair[:, 0:256], matrix(joint, layer, 0))
         partial = partial + dot_nt(grad_pair[:, 128:384], matrix(joint, layer, 1))
         waits = scatter_y(links, scatter_out.at[layer, 3], scatter_in.at[layer, 3], partial)
-        key_weight_grad = dot_tn(normed, grad_pair[:, 0:256])
-        joint_grads[layer, 0] = key_weight_grad.astype(BF16).reshape(4, 4, SHARD, NARROW)
-        value_weight_grad = dot_tn(normed, grad_pair[:, 128:384])
-        joint_grads[layer, 1] = value_weight_grad.astype(BF16).reshape(4, 4, SHARD, NARROW)
+        if layer == 1:
+            joint_gradients()
         sums[layer, 0:1, :] = column_sum(partial * units[layer].reshape(FULL, D))
         sums[layer, 1:2, :] = column_sum(partial)
         sums[layer, 7:8, :] = jnp.concatenate(
@@ -831,6 +843,7 @@
             sums_wait()
             sums_y[y] = sums[s] + sums_cross[...]
             sum_waits.extend(gather_y(links, sums_y))
+            tasks["K0"].first()
         wait_all(waits)
         grad_one = sum_slots(scatter_in.at[layer, 3])
         grad_input = grad_middle + norm_back(grad_one, unit_one, factor_one, gain_one)
@@ -840,7 +853,6 @@
     backward(0, gather_grads(0, in_grads[1]))
     in_grad_wait = links.exchange("s", 1, in_grads.at[other], in_grad_cross, in_grad_cross)
 
-    tasks["K0"].first()
     output_wait()
     activations[s] = outputs[s]
     activations[other] = output_cross[...]

time: 174 us -> 173 us (level)
  no operation moved by 1% of the time
where the time goes in v5:
time: 173 us
  Pallas kernels  172 us (99%)
    pallas_call x1, Pallas kernels, local(): pl.pallas_call(kernel, name='layers', out_shape=(jax.ShapeDtypeStruct((2,...  170 us

profile of v5, /device:TPU:0, one launch (start us, length us, event | category | flops | bytes accessed | tf_op | source)
XLA Modules:
  0.0 172.5 jit_solution(2923423385131611825)
XLA Ops:
  0.7 169.7 %layers.1 = (bf16[2,32,768]{2,1,0:T(8,128)(2,1)}, bf16[2,32,768]{2,1,0:T(8,128)(2,1)}, f32[2,48,768]{2,1,0:T(8,128)}, f32[2,48,256]{2,1,0:T(8,128)}, f32[2,48,256]{2,1,0:T(8,128)}, /*index=5*/f32[8,768]{1,0:T(8,128)}) custom-call(bf16[2,32,768]{2,1,0:T(8,128)(2,1)} %inputs.1, bf16[2,32,768]{2,1,0:T(8,128)(2,1)} %cotangent.1, f32[1,768]{1,0:T(1,128)} %ln1_gain.1, ...), custom_call_target="tpu_custom_call" | custom-call | tf_op jit(solution)/shard_map/layers/pallas_call | solution.py:1022
  170.3 2.0 %results.1 = (bf16[1,2,32,768]{3,2,1,0:T(8,128)(2,1)}, bf16[1,2,32,768]{3,2,1,0:T(8,128)(2,1)}, f32[1,768]{1,0:T(1,128)}, f32[1,768]{1,0:T(1,128)}, f32[1,3,48,1...) custom-call(bf16[2,32,768]{2,1,0:T(8,128)(2,1)} %get-tuple-element.3, ...), custom_call_target="tpu_custom_call" | custom-call | tf_op jit(solution)/shard_map/results/pallas_call | solution.py:1042
